TPU v7x, 32 devices: a whole 2x2x4 slice. The times are simulated.
32 devices in a mesh: dp: 8 (over y, x, core), rep: 4 (over z).
Axes of the slice: x: 2, y: 2, z: 4, core: 2. Of those that a mesh axis runs over, the one named last changes fastest.
Arguments:
- tokens: bfloat16 [32, 1024, 768], P(('dp', 'rep')), may hold values from -6 to 6
- seg_lens: int32 [32, 5], P(('dp', 'rep')), may hold values from 1 to 512, 1024 in all within a row
- cotangent: float32 [32, 1024, 768], P(('dp', 'rep')), may hold values from -6 to 6
- qkv_w: float32 [3, 768, 768], P(None, 'dp'), may hold values from -0.21875 to 0.21875
- out_w: float32 [768, 768], P('dp'), may hold values from -1.25 to 1.25
- gu_w: float32 [2, 768, 2048], P(None, 'dp'), may hold values from -0.21875 to 0.21875
- down_w: float32 [2048, 768], P('dp'), may hold values from -0.25 to 0.25
- gains: float32 [2, 768], P(None, 'dp'), may hold values from 0.5 to 1.5
- qkv_m: float32 [3, 768, 768], P(None, 'dp'), may hold values from -128 to 128
- qkv_v: float32 [3, 768, 768], P(None, 'dp'), may hold values from 851.968 to 6881.28
- out_m: float32 [768, 768], P('dp'), may hold values from -32 to 32
- out_v: float32 [768, 768], P('dp'), may hold values from 75.3664 to 622.592
- gu_m: float32 [2, 768, 2048], P(None, 'dp'), may hold values from -96 to 96
- gu_v: float32 [2, 768, 2048], P(None, 'dp'), may hold values from 557.056 to 4259.84
- down_m: float32 [2048, 768], P('dp'), may hold values from -96 to 96
- down_v: float32 [2048, 768], P('dp'), may hold values from 557.056 to 4259.84
- gain_m: float32 [2, 768], P(None, 'dp'), may hold values from -256 to 256
- gain_v: float32 [2, 768], P(None, 'dp'), may hold values from 3276.8 to 27525.12
Outputs:
- output: float32 [32, 1024, 768], P(('dp', 'rep'))
- input_grad: float32 [32, 1024, 768], P(('dp', 'rep'))
- qkv_moment: float32 [3, 768, 768], P(None, 'dp')
- qkv_second: float32 [3, 768, 768], P(None, 'dp')
- qkv_new: float32 [3, 768, 768], P(None, 'dp')
- out_moment: float32 [768, 768], P('dp')
- out_second: float32 [768, 768], P('dp')
- out_new: float32 [768, 768], P('dp')
- gu_moment: float32 [2, 768, 2048], P(None, 'dp')
- gu_second: float32 [2, 768, 2048], P(None, 'dp')
- gu_new: float32 [2, 768, 2048], P(None, 'dp')
- down_moment: float32 [2048, 768], P('dp')
- down_second: float32 [2048, 768], P('dp')
- down_new: float32 [2048, 768], P('dp')
- gain_moment: float32 [2, 768], P(None, 'dp')
- gain_second: float32 [2, 768], P(None, 'dp')
- gain_new: float32 [2, 768], P(None, 'dp')
Inputs may be any that keep to these rules, and one draw needn't show every extreme that they name: `seg_lens`: each row's 5 lengths are consecutive segments that fill its 1024 slots; the last one is padding; in every draw some segment has exactly 512 slots.
All inputs are finite; a program needn't handle non-finite values.
Results may differ from a plain program's by a relative error of at most 0.014.
The roundings to bfloat16 on the way count: a program that leaves them out, or rounds other values in their place, can miss the bound.
Values may be sent and summed in bfloat16 or wider, within the bound.
A program may use at most 320 MiB of HBM per device.

v0:
```python
import jax
import jax.numpy as jnp
from jax import lax
from jax.sharding import PartitionSpec as P

HEADS = 12
STEP = 10


norm_eps = 1e-05
beta_one = 0.9
beta_two = 0.95
adam_eps = 1e-08
weight_decay = 0.05
matrix_rate = 0.1
gain_rate = 0.3
masked_score = -1e30


def segment_layout(seg_lens, seq_len):
    seg_ends = jnp.cumsum(seg_lens, axis=1)
    seg_starts = seg_ends - seg_lens
    slot_ids = jnp.arange(seq_len, dtype=jnp.int32)
    inside = (
        (slot_ids[None, None, :] >= seg_starts[:, :, None])
        & (slot_ids[None, None, :] < seg_ends[:, :, None])
    ).astype(jnp.int32)
    seg_total = seg_lens.shape[1]
    seg_ids = jnp.sum(inside * jnp.arange(seg_total, dtype=jnp.int32)[None, :, None], axis=1)
    offsets = jnp.sum(inside * seg_starts[:, :, None], axis=1)
    return (seg_ids, slot_ids[None, :] - offsets)


def rope_tables(places, head_size):
    half_len = head_size // 2
    freqs = 10000.0 ** (-jnp.arange(half_len, dtype=jnp.float32) / half_len)
    angles = places.astype(jnp.float32)[:, :, None, None] * freqs
    return (jnp.cos(angles), jnp.sin(angles))


def rotate(tensor, cos_tab, sin_tab):
    half_len = tensor.shape[-1] // 2
    first_half = tensor[..., :half_len]
    second_half = tensor[..., half_len:]
    return jnp.concatenate(
        [
            first_half * cos_tab - second_half * sin_tab,
            second_half * cos_tab + first_half * sin_tab,
        ],
        axis=-1,
    )


def rotate_back(tensor, cos_tab, sin_tab):
    half_len = tensor.shape[-1] // 2
    first_half = tensor[..., :half_len]
    second_half = tensor[..., half_len:]
    return jnp.concatenate(
        [
            first_half * cos_tab + second_half * sin_tab,
            second_half * cos_tab - first_half * sin_tab,
        ],
        axis=-1,
    )


def norm_back(unit_vals, inv_scale, gain_vec, grad_out):
    weighted = grad_out * gain_vec
    inner_mean = jnp.mean(weighted * unit_vals, axis=-1, keepdims=True)
    return (inv_scale * (weighted - unit_vals * inner_mean), jnp.sum(grad_out * unit_vals, axis=0))


def block_mask(seg_row, slot_ids, begin_at, block_len):
    query_seg = seg_row[begin_at : begin_at + block_len]
    query_slot = slot_ids[begin_at : begin_at + block_len]
    return (query_seg[:, None] == seg_row[None, :]) & (slot_ids[None, :] <= query_slot[:, None])


def attend_forward(pieces):
    query_row, key_row, value_row, seg_row = pieces
    seq_len = query_row.shape[0]
    block_len = min(512, seq_len)
    slot_ids = jnp.arange(seq_len, dtype=jnp.int32)
    out_blocks = []
    lse_blocks = []
    for begin_at in range(0, seq_len, block_len):
        allowed = block_mask(seg_row, slot_ids, begin_at, block_len)
        query_blk = query_row[begin_at : begin_at + block_len]
        scores = (
            jnp.einsum("qhd,khd->hqk", query_blk, key_row, preferred_element_type=jnp.float32)
            * 0.125
        )
        scores = jnp.where(allowed[None], scores, masked_score)
        largest = jnp.max(scores, axis=-1, keepdims=True)
        exp_vals = jnp.exp(scores - largest)
        sum_vals = jnp.sum(exp_vals, axis=-1, keepdims=True)
        prob_low = (exp_vals / sum_vals).astype(jnp.bfloat16)
        mixed_blk = jnp.einsum(
            "hqk,khd->qhd", prob_low, value_row, preferred_element_type=jnp.float32
        )
        out_blocks.append(mixed_blk.astype(jnp.bfloat16))
        lse_blocks.append((largest + jnp.log(sum_vals))[..., 0])
    return (jnp.concatenate(out_blocks, axis=0), jnp.concatenate(lse_blocks, axis=1))


def attend_backward(pieces):
    query_row, key_row, value_row, grad_row, seg_row, lse_row = pieces
    seq_len = query_row.shape[0]
    block_len = min(512, seq_len)
    slot_ids = jnp.arange(seq_len, dtype=jnp.int32)
    grad_keys = jnp.zeros(key_row.shape, jnp.float32)
    grad_values = jnp.zeros(value_row.shape, jnp.float32)
    query_blocks = []
    for begin_at in range(0, seq_len, block_len):
        allowed = block_mask(seg_row, slot_ids, begin_at, block_len)
        query_blk = query_row[begin_at : begin_at + block_len]
        grad_blk = grad_row[begin_at : begin_at + block_len]
        lse_blk = lse_row[:, begin_at : begin_at + block_len]
        scores = (
            jnp.einsum("qhd,khd->hqk", query_blk, key_row, preferred_element_type=jnp.float32)
            * 0.125
        )
        scores = jnp.where(allowed[None], scores, masked_score)
        probs = jnp.exp(scores - lse_blk[..., None])
        prob_low = probs.astype(jnp.bfloat16)
        grad_probs = jnp.einsum(
            "qhd,khd->hqk", grad_blk, value_row, preferred_element_type=jnp.float32
        )
        grad_values = grad_values + jnp.einsum(
            "hqk,qhd->khd", prob_low, grad_blk, preferred_element_type=jnp.float32
        )
        inner_sum = jnp.sum(probs * grad_probs, axis=-1, keepdims=True)
        grad_scores = (probs * (grad_probs - inner_sum)).astype(jnp.bfloat16)
        query_blocks.append(
            jnp.einsum("hqk,khd->qhd", grad_scores, key_row, preferred_element_type=jnp.float32)
            * 0.125
        )
        grad_keys = (
            grad_keys
            + jnp.einsum("hqk,qhd->khd", grad_scores, query_blk, preferred_element_type=jnp.float32)
            * 0.125
        )
    return (jnp.concatenate(query_blocks, axis=0), grad_keys, grad_values)


def adam_step(weight, grad_sum, moment, second, rate, decay):
    moment_new = beta_one * moment + (1.0 - beta_one) * grad_sum
    second_new = beta_two * second + (1.0 - beta_two) * grad_sum * grad_sum
    moment_hat = moment_new / (1.0 - beta_one**STEP)
    second_hat = second_new / (1.0 - beta_two**STEP)
    weight_new = weight - rate * (moment_hat / (jnp.sqrt(second_hat) + adam_eps) + decay * weight)
    return (moment_new, second_new, weight_new)


def per_device(
    tokens,
    seg_lens,
    cotangent,
    qkv_w,
    out_w,
    gu_w,
    down_w,
    gains,
    qkv_m,
    qkv_v,
    out_m,
    out_v,
    gu_m,
    gu_v,
    down_m,
    down_v,
    gain_m,
    gain_v,
):
    row_count, seq_len, model_width = tokens.shape
    head_count = HEADS
    head_size = model_width // head_count
    tok_count = row_count * seq_len
    shape_four = (row_count, seq_len, head_count, head_size)
    qkv_full, out_full, gain_full = (
        lax.all_gather(qkv_w.astype(jnp.bfloat16), "dp", axis=1, tiled=True),
        lax.all_gather(out_w.astype(jnp.bfloat16), "dp", axis=0, tiled=True),
        lax.all_gather(gains.astype(jnp.bfloat16), "dp", axis=1, tiled=True),
    )
    gain_one = gain_full[0].astype(jnp.float32)
    gain_two = gain_full[1].astype(jnp.float32)
    seg_ids, places = segment_layout(seg_lens, seq_len)
    cos_tab, sin_tab = rope_tables(places, head_size)
    flat_in = tokens.astype(jnp.float32).reshape(tok_count, model_width)
    scale_one = lax.rsqrt(jnp.mean(flat_in * flat_in, axis=-1, keepdims=True) + norm_eps)
    unit_one = flat_in * scale_one
    normed_one = (unit_one * gain_one).astype(jnp.bfloat16)
    projected = jnp.einsum("td,cde->cte", normed_one, qkv_full, preferred_element_type=jnp.float32)
    query_rot = rotate(projected[0].reshape(shape_four), cos_tab, sin_tab).astype(jnp.bfloat16)
    key_rot = rotate(projected[1].reshape(shape_four), cos_tab, sin_tab).astype(jnp.bfloat16)
    value_low = projected[2].astype(jnp.bfloat16).reshape(shape_four)
    mixed, log_totals = lax.map(attend_forward, (query_rot, key_rot, value_low, seg_ids))
    mixed_flat = mixed.reshape(tok_count, model_width)
    middle = flat_in + jnp.dot(mixed_flat, out_full, preferred_element_type=jnp.float32)
    gu_full, down_full = (
        lax.all_gather(gu_w.astype(jnp.bfloat16), "dp", axis=1, tiled=True),
        lax.all_gather(down_w.astype(jnp.bfloat16), "dp", axis=0, tiled=True),
    )
    scale_two = lax.rsqrt(jnp.mean(middle * middle, axis=-1, keepdims=True) + norm_eps)
    unit_two = middle * scale_two
    normed_two = (unit_two * gain_two).astype(jnp.bfloat16)
    gate_up = jnp.einsum("td,cdf->ctf", normed_two, gu_full, preferred_element_type=jnp.float32)
    gate = gate_up[0]
    upward = gate_up[1]
    silu_gate = jax.nn.silu(gate)
    hidden = (silu_gate * upward).astype(jnp.bfloat16)
    output = middle + jnp.dot(hidden, down_full, preferred_element_type=jnp.float32)
    gu_back, down_back = (
        lax.all_gather(gu_w.astype(jnp.bfloat16), "dp", axis=1, tiled=True),
        lax.all_gather(down_w.astype(jnp.bfloat16), "dp", axis=0, tiled=True),
    )
    grad_top = cotangent.reshape(tok_count, model_width)
    grad_low = grad_top.astype(jnp.bfloat16)
    grad_down = jnp.einsum("tf,td->fd", hidden, grad_low, preferred_element_type=jnp.float32)
    grad_hidden = jnp.einsum("td,fd->tf", grad_low, down_back, preferred_element_type=jnp.float32)
    sig_gate = jax.nn.sigmoid(gate)
    grad_gate = grad_hidden * upward * (sig_gate * (1.0 + gate * (1.0 - sig_gate)))
    grad_upward = grad_hidden * silu_gate
    grad_gu_low = jnp.stack([grad_gate, grad_upward]).astype(jnp.bfloat16)
    grad_gu = jnp.einsum("td,ctf->cdf", normed_two, grad_gu_low, preferred_element_type=jnp.float32)
    grad_normed_two = jnp.einsum(
        "ctf,cdf->td", grad_gu_low, gu_back, preferred_element_type=jnp.float32
    )
    norm_part_two, grad_gain_two = norm_back(unit_two, scale_two, gain_two, grad_normed_two)
    grad_middle = grad_top + norm_part_two
    qkv_back, out_back = (
        lax.all_gather(qkv_w.astype(jnp.bfloat16), "dp", axis=1, tiled=True),
        lax.all_gather(out_w.astype(jnp.bfloat16), "dp", axis=0, tiled=True),
    )
    grad_mid_low = grad_middle.astype(jnp.bfloat16)
    grad_out = jnp.einsum("td,te->de", mixed_flat, grad_mid_low, preferred_element_type=jnp.float32)
    grad_mixed = jnp.einsum(
        "te,de->td", grad_mid_low, out_back, preferred_element_type=jnp.float32
    ).astype(jnp.bfloat16)
    grad_query_rot, grad_key_rot, grad_value = lax.map(
        attend_backward,
        (query_rot, key_rot, value_low, grad_mixed.reshape(shape_four), seg_ids, log_totals),
    )
    grad_query = rotate_back(grad_query_rot, cos_tab, sin_tab).reshape(tok_count, model_width)
    grad_key = rotate_back(grad_key_rot, cos_tab, sin_tab).reshape(tok_count, model_width)
    grad_qkv_low = jnp.stack(
        [grad_query, grad_key, grad_value.reshape(tok_count, model_width)]
    ).astype(jnp.bfloat16)
    grad_qkv = jnp.einsum(
        "td,cte->cde", normed_one, grad_qkv_low, preferred_element_type=jnp.float32
    )
    grad_normed_one = jnp.einsum(
        "cte,cde->td", grad_qkv_low, qkv_back, preferred_element_type=jnp.float32
    )
    norm_part_one, grad_gain_one = norm_back(unit_one, scale_one, gain_one, grad_normed_one)
    input_grad = grad_middle + norm_part_one
    grad_gain = jnp.stack([grad_gain_one, grad_gain_two])
    sum_qkv, sum_out, sum_gain = (
        lax.psum_scatter(grad_qkv, "dp", scatter_dimension=1, tiled=True),
        lax.psum_scatter(grad_out, "dp", scatter_dimension=0, tiled=True),
        lax.psum_scatter(grad_gain, "dp", scatter_dimension=1, tiled=True),
    )
    sum_gu, sum_down = (
        lax.psum_scatter(
            grad_gu.astype(jnp.bfloat16), "dp", scatter_dimension=1, tiled=True
        ).astype(jnp.float32),
        lax.psum_scatter(
            grad_down.astype(jnp.bfloat16), "dp", scatter_dimension=0, tiled=True
        ).astype(jnp.float32),
    )
    sum_qkv, sum_out, sum_gain, sum_gu, sum_down = lax.psum(
        (sum_qkv, sum_out, sum_gain, sum_gu, sum_down), "rep"
    )
    qkv_res = adam_step(qkv_w, sum_qkv, qkv_m, qkv_v, matrix_rate, weight_decay)
    out_res = adam_step(out_w, sum_out, out_m, out_v, matrix_rate, weight_decay)
    gu_res = adam_step(gu_w, sum_gu, gu_m, gu_v, matrix_rate, weight_decay)
    down_res = adam_step(down_w, sum_down, down_m, down_v, matrix_rate, weight_decay)
    gain_res = adam_step(gains, sum_gain, gain_m, gain_v, gain_rate, 0.0)
    states = qkv_res + out_res + gu_res + down_res + gain_res
    return (
        output.reshape(tokens.shape),
        input_grad.reshape(tokens.shape),
        states[0],
        states[1],
        states[2],
        states[3],
        states[4],
        states[5],
        states[6],
        states[7],
        states[8],
        states[9],
        states[10],
        states[11],
        states[12],
        states[13],
        states[14],
    )


def solution(mesh):
    return jax.shard_map(
        per_device,
        mesh=mesh,
        in_specs=(
            P(("dp", "rep"), None, None),
            P(("dp", "rep"), None),
            P(("dp", "rep"), None, None),
            P(None, "dp", None),
            P("dp", None),
            P(None, "dp", None),
            P("dp", None),
            P(None, "dp"),
            P(None, "dp", None),
            P(None, "dp", None),
            P("dp", None),
            P("dp", None),
            P(None, "dp", None),
            P(None, "dp", None),
            P("dp", None),
            P("dp", None),
            P(None, "dp"),
            P(None, "dp"),
        ),
        out_specs=(
            P(("dp", "rep"), None, None),
            P(("dp", "rep"), None, None),
            P(None, "dp", None),
            P(None, "dp", None),
            P(None, "dp", None),
            P("dp", None),
            P("dp", None),
            P("dp", None),
            P(None, "dp", None),
            P(None, "dp", None),
            P(None, "dp", None),
            P("dp", None),
            P("dp", None),
            P("dp", None),
            P(None, "dp"),
            P(None, "dp"),
            P(None, "dp"),
        ),
        check_vma=False,
    )
```

profile of v0, /device:TPU:0, one launch (start us, length us, event | category | flops | bytes accessed | tf_op | source)
XLA Modules:
  0.0 745.0 jit_solution(1057251508817632754)
XLA Ops:
  13.3 10.2 %all-gather = bf16[8,96,2]{1,2,0:T(2,128)(2,1)S(1)} all-gather(bf16[1,96,2]{1,2,0:T(2,128)(2,1)S(1)} %convert_bitcast_fusion.1), channel_id=1, replica_groups=mesh['dp'=8,'rep'=4] {'dp'}, dimensions={0}, use_global_device_ids=true | all-gather | bytes 3456 | tf_op jit(solution)/shard_map/all_gather | solution.py:183
  32.7 14.5 %all-gather.6.cloned.1.call-done = bf16[3,768,768]{2,1,0:T(8,128)(2,1)} async-done(((bf16[3,96,768]{2,1,0:T(8,128)(2,1)}), bf16[3,768,768]{2,1,0:T(8,128)(2,1)}) %all-gather.6.cloned.1.call-update) | async-done | bytes 3538960 | tf_op jit(solution)/shard_map/all_gather | solution.py:181
  56.0 11.3 %fusion.13 = (f32[12,512]{1,0:T(8,128)}, f32[12,512,1024]{2,1,0:T(8,128)}) fusion(pred[512,1024]{1,0:T(8,128)(4,1)S(1)} %get-tuple-element.202, bf16[1024,12,32]{0,2,1:T(8,128)(2,1)S(1)} %get-tuple-element.190, bf16[1024,12,32]{0,2,1:T(8,128)(2,1)S(1)} %get-tuple-element.189, bf16[1,1024,12,32]{1,3,2,0:T(8,128)(2,1)S(1)} %get-tuple-element.197, ...), kind=kOutput, calls=%fused_computation.23 | convolution fusion | flops 828893184 | bytes 28860416 | tf_op jit(solution)/shard_map/while/body/eval_jaxpr/qhd,khd->hqk/dot_general | solution.py:90
  67.3 14.4 %fusion.12 = (f32[12,512]{1,0:T(8,128)}, f32[12,512,1024]{2,1,0:T(8,128)}) fusion(pred[512,1024]{1,0:T(8,128)(4,1)S(1)} %get-tuple-element.201, bf16[1024,12,32]{0,2,1:T(8,128)(2,1)} %copy-done.12, bf16[1024,12,32]{0,2,1:T(8,128)(2,1)} %copy-done.10, bf16[1,1024,12,32]{1,3,2,0:T(8,128)(2,1)} %copy-done.5, bf16[1,1024,12,32]{1,3,2,0:T(8,128)(2,1)} %copy-done.3), kind=kOutput, calls=%fused_computation.22 | convolution fusion | flops 828893184 | bytes 28860416 | tf_op jit(solution)/shard_map/while/body/eval_jaxpr/qhd,khd->hqk/dot_general | solution.py:90
  81.7 13.5 %fusion.1 = f32[12,512]{1,0:T(8,128)S(1)} fusion(f32[12,512]{1,0:T(8,128)} %get-tuple-element.205, f32[12,512,1024]{2,1,0:T(8,128)} %get-tuple-element.206, pred[512,1024]{1,0:T(8,128)(4,1)S(1)} %get-tuple-element.202), kind=kLoop, calls=%fused_computation.13 | loop fusion | flops 25159680 | bytes 25739264 | tf_op jit(solution)/shard_map/while/body/eval_jaxpr/reduce_sum | solution.py:96
  95.3 8.5 %fusion.62 = bf16[512,12,64]{0,2,1:T(8,128)(2,1)} fusion(bf16[1024,12,64]{0,2,1:T(8,128)(2,1)S(1)} %bitcast.208, f32[12,512]{1,0:T(8,128)S(1)} %fusion.1, f32[12,512]{1,0:T(8,128)S(1)} %copy-done.35, f32[12,512,1024]{2,1,0:T(8,128)S(1)} %bitcast.205, pred[512,1024]{1,0:T(8,128)(4,1)S(1)} %get-tuple-element.202), kind=kOutput, calls=%fused_computation.117 | convolution fusion | flops 837156864 | bytes 28098560 | tf_op jit(solution)/shard_map/while/body/eval_jaxpr/hqk,khd->qhd/dot_general | solution.py:98
  103.8 13.5 %fusion = f32[12,512]{1,0:T(8,128)S(1)} fusion(f32[12,512]{1,0:T(8,128)} %get-tuple-element.207, f32[12,512,1024]{2,1,0:T(8,128)} %get-tuple-element.208, pred[512,1024]{1,0:T(8,128)(4,1)S(1)} %get-tuple-element.201), kind=kLoop, calls=%fused_computation.12 | loop fusion | flops 25159680 | bytes 25739264 | tf_op jit(solution)/shard_map/while/body/eval_jaxpr/reduce_sum | solution.py:96
  134.7 13.7 %convolution_bitcast_fusion = f32[2,1024,2048]{2,1,0:T(8,128)} fusion(bf16[2,768,2048]{2,1,0:T(8,128)(2,1)} %all-gather.10.cloned.1.call-done, f32[1024,768]{0,1:T(8,128)} %get-tuple-element.210, f32[768]{0:T(1024)S(1)} %copy-done.41, f32[1024]{0:T(1024)S(1)} %add_rsqrt_fusion), kind=kOutput, calls=%fused_computation.40 | convolution fusion | flops 6444810240 | bytes 26221568 | tf_op jit(solution)/shard_map/td,cdf->ctf/dot_general | solution.py:207
  148.4 8.1 %all-gather.12.cloned.1.call-done = bf16[2048,768]{1,0:T(8,128)(2,1)} async-done(((bf16[256,768]{1,0:T(8,128)(2,1)}), bf16[2048,768]{1,0:T(8,128)(2,1)}) %all-gather.12.cloned.1.call-update) | async-done | bytes 3145744 | tf_op jit(solution)/shard_map/all_gather | solution.py:202
  156.5 14.9 %fusion.33 = (bf16[1,1024,2048]{2,1,0:T(8,128)(2,1)}, bf16[1,1024,2048]{2,1,0:T(8,128)(2,1)}) fusion(f32[2,1024,2048]{2,1,0:T(8,128)} %convolution_bitcast_fusion, bf16[2048,768]{1,0:T(8,128)(2,1)} %all-gather.12.cloned.1.call-done, f32[1,1024,768]{1,2,0:T(8,128)} %copy.173), kind=kOutput, calls=%fused_computation.56 | convolution fusion | flops 3248488448 | bytes 31457280 | tf_op jit(solution)/shard_map/td,fd->tf/dot_general | solution.py:220
  171.5 11.8 %convert_bitcast_fusion = bf16[2,768,2048]{1,2,0:T(8,128)(2,1)} fusion(bf16[1,1024,2048]{2,1,0:T(8,128)(2,1)} %get-tuple-element.182, bf16[1,1024,2048]{2,1,0:T(8,128)(2,1)} %get-tuple-element.181, f32[1024,768]{0,1:T(8,128)S(1)} %copy-done.17, f32[768]{0:T(1024)S(1)} %copy-done.41, f32[1024]{0:T(1024)S(1)} %add_rsqrt_fusion), kind=kOutput, calls=%fused_computation.41 | convolution fusion | flops 6452150272 | bytes 17832960 | tf_op jit(solution)/shard_map/td,ctf->cdf/dot_general | solution.py:225
  183.4 10.1 %fusion.45 = (f32[768]{0:T(1024)}, f32[1024]{0:T(1024)S(1)}, f32[1024,768,1]{0,1,2:T(8,128)S(1)}) fusion(f32[1024,768]{0,1:T(8,128)S(1)} %copy-done.17, f32[1024]{0:T(1024)S(1)} %add_rsqrt_fusion, f32[768]{0:T(1024)S(1)} %copy-done.41, bf16[2,768,2048]{2,1,0:T(8,128)(2,1)S(1)} %bitcast.232, bf16[1,1024,2048]{2,1,0:T(8,128)(2,1)} %get-tuple-element.182, ...), kind=kOutput, calls=%fused_computation.72 | convolution fusion | flops 6451361792 | bytes 20985856 | tf_op jit(solution)/shard_map/ctf,cdf->td/dot_general | solution.py:226
  197.4 13.1 %fusion.4 = f32[12,64,1024]{2,1,0:T(8,128)} fusion(bf16[512,12,64]{0,2,1:T(8,128)(2,1)S(1)} %bitcast.219, f32[12,512]{1,0:T(8,128)S(1)} %log_add_fusion, f32[12,512,1024]{2,1,0:T(8,128)} %get-tuple-element.206, pred[512,1024]{1,0:T(8,128)(4,1)S(1)} %get-tuple-element.202), kind=kOutput, calls=%fused_computation.16 | convolution fusion | flops 830472192 | bytes 29646848 | tf_op jit(solution)/shard_map/while/body/eval_jaxpr/hqk,qhd->khd/dot_general | solution.py:129
  210.5 18.1 %multiply_reduce_fusion = (f32[12,512]{1,0:T(8,128)S(1)}, f32[12,512,1024]{2,1,0:T(8,128)}) fusion(f32[12,512]{1,0:T(8,128)S(1)} %log_add_fusion, f32[12,512,1024]{2,1,0:T(8,128)} %get-tuple-element.206, pred[512,1024]{1,0:T(8,128)(4,1)S(1)} %get-tuple-element.202, bf16[512,12,64]{0,2,1:T(8,128)(2,1)} %bitcast.220, bf16[1024,12,64]{0,2,1:T(8,128)(2,1)S(1)} %bitcast.210), kind=kOutput, calls=%fused_computation.1 | convolution fusion | flops 836757504 | bytes 53264384 | tf_op jit(solution)/shard_map/while/body/eval_jaxpr/qhd,khd->hqk/dot_general | solution.py:126
  228.7 16.4 %copy.184 = bf16[2,768,2048]{2,0,1:T(2,128)(2,1)} copy(bf16[2,768,2048]{1,2,0:T(8,128)(2,1)} %convert_bitcast_fusion) | data formatting | bytes 12582912 | tf_op jit(solution)/shard_map/convert_element_type | solution.py:265
  245.1 22.3 %multiply_reduce_fusion.1 = (f32[12,512]{1,0:T(8,128)}, f32[12,512,1024]{2,1,0:T(8,128)}) fusion(f32[12,512]{1,0:T(8,128)S(1)} %log_add_fusion.1, f32[12,512,1024]{2,1,0:T(8,128)} %get-tuple-element.208, pred[512,1024]{1,0:T(8,128)(4,1)S(1)} %get-tuple-element.201, bf16[512,12,64]{0,2,1:T(8,128)(2,1)S(1)} %bitcast.217, bf16[1024,12,64]{0,2,1:T(8,128)(2,1)S(1)} %bitcast.211), kind=kOutput, calls=%fused_computation.4 | convolution fusion | flops 836757504 | bytes 53264384 | tf_op jit(solution)/shard_map/while/body/eval_jaxpr/qhd,khd->hqk/dot_general | solution.py:126
  267.4 14.2 %add_convert_fusion = bf16[12,64,1024]{2,1,0:T(8,128)(2,1)} fusion(f32[12,64,1024]{2,1,0:T(8,128)} %fusion.4, bf16[512,12,64]{0,2,1:T(8,128)(2,1)S(1)} %bitcast.218, f32[12,512]{1,0:T(8,128)S(1)} %log_add_fusion.1, f32[12,512,1024]{2,1,0:T(8,128)} %get-tuple-element.208, pred[512,1024]{1,0:T(8,128)(4,1)S(1)} %get-tuple-element.201), kind=kOutput, calls=%fused_computation.75 | convolution fusion | flops 832045056 | bytes 31219712 | tf_op jit(solution)/shard_map/while/body/eval_jaxpr/hqk,qhd->khd/dot_general | solution.py:129
  281.6 43.6 %multiply_convert_fusion = (bf16[12,512,1024]{2,1,0:T(8,128)(2,1)}, bf16[12,512,1024]{2,1,0:T(8,128)(2,1)}) fusion(f32[12,512,1024]{2,1,0:T(8,128)} %get-tuple-element.213, f32[12,512]{1,0:T(8,128)S(1)} %get-tuple-element.212, f32[12,512]{1,0:T(8,128)S(1)} %log_add_fusion, f32[12,512,1024]{2,1,0:T(8,128)} %get-tuple-element.206, ...), kind=kLoop, calls=%fused_computation | loop fusion | flops 75497472 | bytes 126976000 | tf_op jit(solution)/shard_map/while/body/eval_jaxpr/convert_element_type | solution.py:133
  325.2 8.8 %multiply_bitcast_fusion.1 = f32[512,12,64]{0,2,1:T(8,128)S(1)} fusion(bf16[12,512,1024]{2,1,0:T(8,128)(2,1)} %get-tuple-element.217, bf16[1024,12,32]{0,2,1:T(8,128)(2,1)S(1)} %copy-done.13, bf16[1024,12,32]{0,2,1:T(8,128)(2,1)S(1)} %copy-done.11), kind=kOutput, calls=%fused_computation.107 | convolution fusion | flops 808845312 | bytes 15728640 | tf_op jit(solution)/shard_map/while/body/eval_jaxpr/hqk,khd->qhd/dot_general | solution.py:135
  334.0 8.8 %multiply_bitcast_fusion.2 = f32[512,12,64]{0,2,1:T(8,128)S(1)} fusion(bf16[12,512,1024]{2,1,0:T(8,128)(2,1)} %get-tuple-element.218, bf16[1024,12,32]{0,2,1:T(8,128)(2,1)S(1)} %copy-done.13, bf16[1024,12,32]{0,2,1:T(8,128)(2,1)S(1)} %copy-done.11), kind=kOutput, calls=%fused_computation.108 | convolution fusion | flops 808845312 | bytes 15728640 | tf_op jit(solution)/shard_map/while/body/eval_jaxpr/hqk,khd->qhd/dot_general | solution.py:135
  367.8 9.3 %convolution_bitcast_fusion.2 = f32[3,768,768]{1,2,0:T(8,128)} fusion(bf16[1,1024,768]{2,1,0:T(8,128)(2,1)} %copy.177, bf16[1,1024,768]{2,1,0:T(8,128)(2,1)} %copy.176, bf16[1,1024,768]{2,1,0:T(8,128)(2,1)} %copy.175, bf16[1,1024,768]{1,2,0:T(8,128)(2,1)S(1)} %copy-done.2, f32[768]{0:T(1024)S(1)} %copy-done.43, f32[1024]{0:T(1024)S(1)} %copy-done.45), kind=kOutput, calls=%fused_computation.81 | convolution fusion | flops 3631742976 | bytes 13376512 | tf_op jit(solution)/shard_map/td,cte->cde/dot_general | solution.py:249
  377.1 11.0 %copy.207 = f32[3,768,768]{2,0,1:T(4,128)} copy(f32[3,768,768]{1,2,0:T(8,128)} %convolution_bitcast_fusion.2) | data formatting | bytes 14155776
  388.2 8.2 %copy.212 = f32[96,8,3,768]{3,1,2,0:T(8,128)} copy(f32[96,8,3,768]{3,2,1,0:T(4,128)} %bitcast.206) | data formatting | bytes 14155776
  402.6 10.1 %fusion.43 = (f32[768]{0:T(1024)S(1)}, f32[1024]{0:T(1024)S(1)}, f32[1024,768,1]{0,1,2:T(8,128)}) fusion(bf16[1,1024,768]{1,2,0:T(8,128)(2,1)S(1)} %copy-done.2, f32[1024]{0:T(1024)S(1)} %copy-done.45, f32[768]{0:T(1024)S(1)} %copy-done.43, bf16[3,768,768]{2,1,0:T(8,128)(2,1)} %all-gather.6.cloned.1.call-done, bf16[1,1024,768]{2,1,0:T(8,128)(2,1)} %copy.177, ...), kind=kOutput, calls=%fused_computation.65 | convolution fusion | flops 3634100480 | bytes 12990464 | tf_op jit(solution)/shard_map/cte,cde->td/dot_general | solution.py:252
  414.0 12.8 %fusion.34 = bf16[2048,768]{1,0:T(8,128)(2,1)} fusion(f32[2,1024,2048]{2,1,0:T(8,128)} %convolution_bitcast_fusion, f32[1,1024,768]{2,1,0:T(8,128)} %param.20), kind=kOutput, calls=%fused_computation.58 | convolution fusion | flops 3236167680 | bytes 23068672 | tf_op jit(solution)/shard_map/tf,td->fd/dot_general | solution.py:219
  431.8 30.4 %reduce-scatter.13.cloned.1.call-done = f32[96,2304]{1,0:T(8,128)} async-done(((f32[768,2304]{1,0:T(8,128)}), f32[96,2304]{1,0:T(8,128)}) %reduce-scatter.13.cloned.1.call-update) | async-done | bytes 884752
  464.9 43.7 %reduce-scatter.9.cloned.1.call-done = f32[96,768]{1,0:T(8,128)} async-done(((f32[768,768]{1,0:T(8,128)}), f32[96,768]{1,0:T(8,128)}) %reduce-scatter.9.cloned.1.call-update) | async-done | bytes 294928 | tf_op jit(solution)/shard_map/reduce_scatter | solution.py:260
  508.7 12.8 %add_bitcast_fusion = f32[1,1024,768]{1,2,0:T(8,128)} fusion(f32[1024,768]{0,1:T(8,128)} %get-tuple-element.210, bf16[2048,768]{1,0:T(8,128)(2,1)} %all-gather.12.cloned.1.call-done, f32[2,1024,2048]{2,1,0:T(8,128)} %convolution_bitcast_fusion), kind=kOutput, calls=%fused_computation.78 | convolution fusion | flops 3234594816 | bytes 26214400 | tf_op jit(solution)/shard_map/dot_general | solution.py:212
  534.0 12.4 %reduce-scatter.15.cloned.1.call-done = f32[96,2]{1,0:T(8,128)} async-done(((f32[768,2]{1,0:T(8,128)}), f32[96,2]{1,0:T(8,128)}) %reduce-scatter.15.cloned.1.call-update) | async-done | bytes 784
  547.3 49.2 %reduce-scatter.11.cloned.1.call-done = bf16[256,768]{1,0:T(8,128)(2,1)} async-done(((bf16[2048,768]{1,0:T(8,128)(2,1)}), bf16[256,768]{1,0:T(8,128)(2,1)}) %reduce-scatter.11.cloned.1.call-update) | async-done | bytes 393232 | tf_op jit(solution)/shard_map/reduce_scatter | solution.py:267
  596.5 60.8 %all-reduce.10 = (f32[256,768]{1,0:T(8,128)}, f32[2,96]{1,0:T(2,128)S(1)}) all-reduce(bf16[256,768]{1,0:T(8,128)(2,1)} %reduce-scatter.11.cloned.1.call-done, f32[2,96]{1,0:T(2,128)S(1)} %copy.210), channel_id=1, replica_groups=mesh['dp'=8,'rep'=4] {'rep'}, use_global_device_ids=true, to_apply=%region_20.21 | all-reduce | flops 196800 | bytes 1181184 | tf_op jit(solution)/shard_map/psum | solution.py:271
  661.4 67.5 %all-reduce.9.cloned.1.call-done = (f32[3,96,768]{2,1,0:T(8,128)}, f32[96,768]{1,0:T(8,128)}, f32[2,96,2048]{2,1,0:T(8,128)}) async-done(((f32[3,96,768]{2,1,0:T(8,128)}, f32[96,768]{1,0:T(8,128)}, f32[2,96,2048]{2,1,0:T(8,128)}), (f32[3,96,768]{2,1,0:T(8,128)}, f32[96,768]{1,0:T(8,128)}, f32[2,96,2048]{2,1,0:T(8,128)})) %all-reduce.9.cloned.1.call-update) | async-done | bytes 2752528 | tf_op jit(solution)/shard_map/psum | solution.py:271
  (218 shorter events, 110.7 us)
Async XLA Ops:
  7.2 40.0 %all-gather.6.cloned.1.call-start = ((), (), s32[]{:S(2)}) async-start(), calls=%async_computation.4 | async-start | bytes 3981312 | tf_op jit(solution)/shard_map/all_gather | solution.py:181
  9.4 119.6 %all-gather.8.cloned.1.call-start = ((), (), s32[]{:S(2)}) async-start(), calls=%async_computation.5 | async-start | bytes 1327104 | tf_op jit(solution)/shard_map/all_gather | solution.py:182
  11.1 123.5 %all-gather.10.cloned.1.call-start = ((), (), s32[]{:S(2)}) async-start(), calls=%async_computation.6 | async-start | bytes 7077888 | tf_op jit(solution)/shard_map/all_gather | solution.py:201
  12.2 144.3 %all-gather.12.cloned.1.call-start = ((), (), s32[]{:S(2)}) async-start(), calls=%async_computation.7 | async-start | bytes 3538944 | tf_op jit(solution)/shard_map/all_gather | solution.py:202
  13.1 415.6 %all-reduce.7.cloned.1.call-start = ((), (), s32[]{:S(2)}) async-start(), calls=%async_computation.12 | async-start | bytes 12582912
  24.3 22.9 %copy-start.42 = (f32[768]{0:T(1024)}, f32[768]{0:T(1024)S(1)}, u32[]{:S(2)}) copy-start(f32[768]{0:T(1024)S(1)} %get-tuple-element.158) | copy-start | bytes 9220
  26.2 21.0 %copy-start.1 = (bf16[1,1024,768]{1,2,0:T(8,128)(2,1)}, bf16[1,1024,768]{1,2,0:T(8,128)(2,1)S(1)}, u32[]{:S(2)}) copy-start(bf16[1,1024,768]{1,2,0:T(8,128)(2,1)S(1)} %copy.168) | copy-start | bytes 4718596
  26.6 20.7 %copy-start.44 = (f32[1024]{0:T(1024)}, f32[1024]{0:T(1024)S(1)}, u32[]{:S(2)}) copy-start(f32[1024]{0:T(1024)S(1)} %add_rsqrt_fusion.1) | copy-start | bytes 12292
  67.2 28.0 %slice-start = ((s8[25165824]{0:T(1024)(128)(4,1)}), s8[4194304]{0:T(1024)(128)(4,1)S(1)}, s32[]{:S(2)}) async-start(s8[25165824]{0:T(1024)(128)(4,1)} %bitcast.204), calls=%async_computation.14 | async-start | bytes 8388608
  67.3 28.0 %slice-start.1 = ((s8[25165824]{0:T(1024)(128)(4,1)}), s8[4194304]{0:T(1024)(128)(4,1)S(1)}, s32[]{:S(2)}) async-start(s8[25165824]{0:T(1024)(128)(4,1)} %bitcast.204), calls=%async_computation.15 | async-start | bytes 8388608
  67.3 28.0 %slice-start.2 = ((s8[25165824]{0:T(1024)(128)(4,1)}), s8[4194304]{0:T(1024)(128)(4,1)S(1)}, s32[]{:S(2)}) async-start(s8[25165824]{0:T(1024)(128)(4,1)} %bitcast.204), calls=%async_computation.16 | async-start | bytes 8388608
  67.3 28.0 %slice-start.3 = ((s8[25165824]{0:T(1024)(128)(4,1)}), s8[4194304]{0:T(1024)(128)(4,1)S(1)}, s32[]{:S(2)}) async-start(s8[25165824]{0:T(1024)(128)(4,1)} %bitcast.204), calls=%async_computation.17 | async-start | bytes 8388608
  103.8 15.9 %copy-start = (f32[12,512,1024]{2,1,0:T(8,128)S(1)}, f32[12,512,1024]{2,1,0:T(8,128)}, u32[]{:S(2)}) copy-start(f32[12,512,1024]{2,1,0:T(8,128)} %get-tuple-element.208) | copy-start | bytes 75497472
  103.8 15.9 %copy-start.38 = (f32[12,512]{1,0:T(8,128)S(1)}, f32[12,512]{1,0:T(8,128)}, u32[]{:S(2)}) copy-start(f32[12,512]{1,0:T(8,128)} %get-tuple-element.207) | copy-start | bytes 73732
  156.5 14.9 %copy-start.17 = (f32[1024,768]{0,1:T(8,128)S(1)}, f32[1024,768]{0,1:T(8,128)}, u32[]{:S(2)}) copy-start(f32[1024,768]{0,1:T(8,128)} %get-tuple-element.210) | copy-start | bytes 9437188
  156.5 26.8 %slice-start.6 = ((s8[6291456]{0:T(1024)(128)(4,1)}), s8[4194304]{0:T(1024)(128)(4,1)S(1)}, s32[]{:S(2)}) async-start(s8[6291456]{0:T(1024)(128)(4,1)} %bitcast.231), calls=%async_computation.20 | async-start | bytes 8388608
  245.1 217.1 %reduce-scatter.13.cloned.1.call-start = ((), (), s32[]{:S(2)}) async-start(), calls=%async_computation.10 | async-start | bytes 7962624
  281.6 43.6 %copy-start.11 = (bf16[1024,12,32]{0,2,1:T(8,128)(2,1)S(1)}, bf16[1024,12,32]{0,2,1:T(8,128)(2,1)}, u32[]{:S(2)}) copy-start(bf16[1024,12,32]{0,2,1:T(8,128)(2,1)} %copy-done.10) | copy-start | bytes 2359300
  281.6 43.6 %copy-start.13 = (bf16[1024,12,32]{0,2,1:T(8,128)(2,1)S(1)}, bf16[1024,12,32]{0,2,1:T(8,128)(2,1)}, u32[]{:S(2)}) copy-start(bf16[1024,12,32]{0,2,1:T(8,128)(2,1)} %copy-done.12) | copy-start | bytes 2359300
  396.4 112.2 %reduce-scatter.9.cloned.1.call-start = ((), (), s32[]{:S(2)}) async-start(), calls=%async_computation.8 | async-start | bytes 2654208 | tf_op jit(solution)/shard_map/reduce_scatter | solution.py:260
  402.5 143.9 %reduce-scatter.15.cloned.1.call-start = ((), (), s32[]{:S(2)}) async-start(), calls=%async_computation.11 | async-start | bytes 442368
  413.7 182.8 %reduce-scatter.11.cloned.1.call-start = ((), (), s32[]{:S(2)}) async-start(), calls=%async_computation.9 | async-start | bytes 3538944 | tf_op jit(solution)/shard_map/reduce_scatter | solution.py:267
  426.8 302.2 %all-reduce.9.cloned.1.call-start = ((), (), s32[]{:S(2)}) async-start(), calls=%async_computation.13 | async-start | bytes 5505024 | tf_op jit(solution)/shard_map/psum | solution.py:271
  530.4 126.9 %copy-start.48 = (f32[2,96]{1,0:T(2,128)S(1)}, f32[2,96]{1,0:T(2,128)}, u32[]{:S(2)}) copy-start(f32[2,96]{1,0:T(2,128)} %param.25) | copy-start | bytes 2308
  530.4 126.9 %copy-start.49 = (f32[2,96]{1,0:T(2,128)S(1)}, f32[2,96]{1,0:T(2,128)}, u32[]{:S(2)}) copy-start(f32[2,96]{1,0:T(2,128)} %param.35) | copy-start | bytes 2308
  530.4 126.9 %copy-start.50 = (f32[2,96]{1,0:T(2,128)S(1)}, f32[2,96]{1,0:T(2,128)}, u32[]{:S(2)}) copy-start(f32[2,96]{1,0:T(2,128)} %param.34) | copy-start | bytes 2308
  530.4 127.5 %copy-start.19 = (f32[256,768]{1,0:T(8,128)S(1)}, f32[256,768]{1,0:T(8,128)}, u32[]{:S(2)}) copy-start(f32[256,768]{1,0:T(8,128)} %param.24) | copy-start | bytes 2359300
  534.0 194.9 %copy-start.30 = (f32[96,768]{1,0:T(8,128)S(1)}, f32[96,768]{1,0:T(8,128)}, u32[]{:S(2)}) copy-start(f32[96,768]{1,0:T(8,128)} %param.22) | copy-start | bytes 884740
  534.0 194.9 %copy-start.33 = (f32[96,768]{1,0:T(8,128)S(1)}, f32[96,768]{1,0:T(8,128)}, u32[]{:S(2)}) copy-start(f32[96,768]{1,0:T(8,128)} %param.29) | copy-start | bytes 884740
  534.0 194.9 %copy-start.34 = (f32[96,768]{1,0:T(8,128)S(1)}, f32[96,768]{1,0:T(8,128)}, u32[]{:S(2)}) copy-start(f32[96,768]{1,0:T(8,128)} %param.28) | copy-start | bytes 884740
  657.9 73.2 %copy-start.16 = (f32[3,96,768]{2,1,0:T(8,128)S(1)}, f32[3,96,768]{2,1,0:T(8,128)}, u32[]{:S(2)}) copy-start(f32[3,96,768]{2,1,0:T(8,128)} %param.21) | copy-start | bytes 2654212
  657.9 73.2 %copy-start.31 = (f32[3,96,768]{2,1,0:T(8,128)S(1)}, f32[3,96,768]{2,1,0:T(8,128)}, u32[]{:S(2)}) copy-start(f32[3,96,768]{2,1,0:T(8,128)} %param.27) | copy-start | bytes 2654212
  (41 other events, 251.5 us)
Sparse Core Ops, SparseCore 0:
  10.5 36.6 all-gather.5
  49.7 24.0 all-gather.7
  76.3 45.5 all-gather.9
  124.1 32.3 all-gather.11
  245.2 104.1 all-reduce.6
  396.5 65.6 reduce-scatter.12
  466.2 42.4 reduce-scatter.8
  512.6 33.8 reduce-scatter.14
  550.2 46.2 reduce-scatter.10
  600.0 128.8 all-reduce.8
where the time goes:
time: 755 us; the launch traced here: 745 us
  matrix products  255 us (34%)
  waiting for transfers between devices  226 us (30%)
  other arithmetic  109 us (14%)
  blocking collectives  71 us (9%)
  local copies, waits for them, and re-layouts  67.7 us (9%)
  between operations  16 us (2%)
    psum x1, waiting for transfers between devices, per_device(): lax.psum((sum_qkv, sum_out, sum_gain, sum_gu, sum_down), 'rep')  67.5 us
    psum x1, blocking collectives, per_device(): lax.psum((sum_qkv, sum_out, sum_gain, sum_gu, sum_down), 'rep')  60.8 us
    reduce_scatter x1, waiting for transfers between devices, per_device(): lax.psum_scatter(grad_down.astype(jnp.bfloat16), 'dp', scatter_dimension=...  49.2 us
    unnamed x138, local copies, waits for them, and re-layouts  43.8 us
    reduce_scatter x1, waiting for transfers between devices, per_device(): lax.psum_scatter(grad_out, 'dp', scatter_dimension=0, tiled=True)  43.7 us
    convert_element_type x1, other arithmetic, attend_backward(): grad_scores = (probs * (grad_probs - inner_sum)).astype(jnp.bfloat16)  43.6 us
    unnamed x13, waiting for transfers between devices  43 us
    dot_general x2, matrix products, attend_backward(): jnp.einsum('qhd,khd->hqk', grad_blk, value_row, preferred_element_type=jn...  40.4 us
  transfers between devices with their start and end apart: 10, of which 7 were waited for; matrix products, arithmetic and copies ran while one was open for 44% of the time, Pallas kernels for 0%

commit v1 on v0

v1 whole, which is shorter than its diff:
```python
import functools

import jax
import jax.numpy as jnp
from jax import lax
from jax.experimental import pallas as pl
from jax.experimental.pallas import tpu as pltpu
from jax.sharding import PartitionSpec as P

bf16, f32 = jnp.bfloat16, jnp.float32
STEP = 10
beta_one, beta_two, adam_eps = 0.9, 0.95, 1e-08
weight_decay, matrix_rate, gain_rate = 0.05, 0.1, 0.3
EPS = 1e-5
def nn(a,b): return lax.dot_general(a,b,(((1,),(0,)),((),())),preferred_element_type=f32)
def nt(a,b): return lax.dot_general(a,b,(((1,),(1,)),((),())),preferred_element_type=f32)
def tn(a,b): return lax.dot_general(a,b,(((0,),(0,)),((),())),preferred_element_type=f32)

def mlp_kernel(T, x_ref, ob_ref, obT_ref, cot_ref, wo_ref, wgu_ref, wd_ref, gain_ref,
               out_ref, dmid_ref, dob_ref, dobT_ref, dwo_ref, dwgu_ref, dwd_ref,
               h2_s, h2T_s, dfb_s, dh2_s, r_s, hid_s, dg_s, du_s):
    f = pl.program_id(0); nf = pl.num_programs(0)
    S = x_ref.shape[0]; nt_ = S // T
    gain = gain_ref[1:2, :]
    @pl.when(f == 0)
    def _():
        @pl.loop(0, nt_)
        def _(i):
            t = pl.ds(pl.multiple_of(i*T, T), T)
            mid = x_ref[t, :].astype(f32) + nn(ob_ref[t, :], wo_ref[...])
            out_ref[t, :] = mid
            dmid_ref[t, :] = mid
            r = lax.rsqrt(jnp.mean(mid*mid, axis=-1, keepdims=True) + EPS)
            r_s[t, :] = jnp.broadcast_to(r, (T, 128))
            h2 = ((mid*r)*gain).astype(bf16)
            h2_s[t, :] = h2
            h2T_s[:, t] = h2.T
            dfb_s[t, :] = cot_ref[t, :].astype(bf16)
            dh2_s[t, :] = jnp.zeros_like(mid)
    @pl.loop(0, nt_)
    def _(i):
        t = pl.ds(pl.multiple_of(i*T, T), T)
        h2 = h2_s[t, :]; dfb = dfb_s[t, :]
        g = nn(h2, wgu_ref[0]); u = nn(h2, wgu_ref[1])
        dh = nt(dfb, wd_ref[...])
        sig = 0.5*jnp.tanh(0.5*g)+0.5
        silu = g*sig
        hid = (silu*u).astype(bf16)
        dg = (dh*u*(sig*(1.0+g*(1.0-sig)))).astype(bf16)
        du = (dh*silu).astype(bf16)
        hid_s[t, :] = hid; dg_s[t, :] = dg; du_s[t, :] = du
        out_ref[t, :] += nn(hid, wd_ref[...])
        dh2_s[t, :] += nt(dg, wgu_ref[0]) + nt(du, wgu_ref[1])
    dwd_ref[...] = tn(hid_s[...], dfb_s[...]).astype(bf16)
    dwgu_ref[0] = nn(h2T_s[...], dg_s[...]).astype(bf16)
    dwgu_ref[1] = nn(h2T_s[...], du_s[...]).astype(bf16)
    @pl.when(f == nf-1)
    def _():
        @pl.loop(0, nt_)
        def _(i):
            t = pl.ds(pl.multiple_of(i*T, T), T)
            mid = dmid_ref[t, :]; r = r_s[t, 0:1]
            xh = mid*r; dh = dh2_s[t, :]; w = dh*gain
            back = r*(w - xh*jnp.mean(w*xh, axis=-1, keepdims=True))
            dmid = cot_ref[t, :] + back
            dmid_ref[t, :] = dmid
            dab = dmid.astype(bf16)
            h2_s[t, :] = dab
            dob_ref[t, :] = nt(dab, wo_ref[...]).astype(bf16)
            dobT_ref[:, t] = nt(wo_ref[...], dab).astype(bf16)
        dwo_ref[...] = nn(obT_ref[...], h2_s[...]).astype(bf16)

def mlp(x, ob, obT, cot, wo, wgu, wd, gains, FC=512, T=256):
    S, D = x.shape; FF = wd.shape[0]
    full = lambda *s: pl.BlockSpec(s, lambda f: (0,)*len(s), pipeline_mode=pl.Buffered(1))
    return pl.pallas_call(
        functools.partial(mlp_kernel, T), grid=(FF//FC,),
        in_specs=[full(S,D), full(S,D), full(D,S), full(S,D), full(D,D),
                  pl.BlockSpec((2,D,FC), lambda f:(0,0,f)), pl.BlockSpec((FC,D), lambda f:(f,0)), full(8,D)],
        out_specs=[full(S,D), full(S,D), full(S,D), full(D,S), full(D,D),
                  pl.BlockSpec((2,D,FC), lambda f:(0,0,f)), pl.BlockSpec((FC,D), lambda f:(f,0))],
        out_shape=[jax.ShapeDtypeStruct((S,D),f32), jax.ShapeDtypeStruct((S,D),f32), jax.ShapeDtypeStruct((S,D),bf16),
                   jax.ShapeDtypeStruct((D,S),bf16), jax.ShapeDtypeStruct((D,D),bf16),
                   jax.ShapeDtypeStruct((2,D,FF),bf16), jax.ShapeDtypeStruct((FF,D),bf16)],
        scratch_shapes=[pltpu.VMEM((S,D),bf16), pltpu.VMEM((D,S),bf16), pltpu.VMEM((S,D),bf16), pltpu.VMEM((S,D),f32),
                        pltpu.VMEM((S,128),f32), pltpu.VMEM((S,FC),bf16), pltpu.VMEM((S,FC),bf16), pltpu.VMEM((S,FC),bf16)],
        compiler_params=pltpu.CompilerParams(vmem_limit_bytes=62*2**20),
        name="mlp",
    )(x, ob, obT, cot, wo, wgu, wd, gains)
H, HD = 12, 64
NEG = -1e30
VM = pl.BlockSpec(memory_space=pltpu.VMEM)
def tnt(a,b): return lax.dot_general(a,b,(((0,),(1,)),((),())),preferred_element_type=f32)

def seg_rows(lens_ref, S):
    slot = lax.broadcasted_iota(jnp.int32, (8, S), 1)
    seg = jnp.zeros((8, S), jnp.int32); start = jnp.zeros((8, S), jnp.int32)
    end = jnp.int32(0)
    for s in range(lens_ref.shape[1]-1):
        end = end + lens_ref[0, s]
        past = (slot >= end).astype(jnp.int32)
        seg += past
        start += past * lens_ref[0, s]
    return seg, slot - start

def attn_fwd_body(lens_ref, x_ref, gain_ref, freq_ref, wqkv_ref, qT_ref, kT_ref, vT_ref, ob_ref, oT_ref, lse_ref, cos_ref, sin_ref, segc_ref, segr_ref,
                 bias_s, B=256):
    S, D = x_ref.shape
    n = S // B
    seg, place = seg_rows(lens_ref, S)
    ang = jnp.broadcast_to(place[0:1, :].astype(f32), (HD//2, S)) * freq_ref[:, 0:1]
    cos_ref[...] = jnp.cos(ang); sin_ref[...] = jnp.sin(ang)
    segf = jnp.broadcast_to(seg[0:1, :].astype(f32), (128, S))
    segr_ref[...] = segf[0:8]
    segc_ref[...] = segf.T
    @pl.loop(0, n)
    def _(i):
        t = pl.ds(pl.multiple_of(i*B, B), B)
        xf = x_ref[t, :].astype(f32)
        r = lax.rsqrt(jnp.mean(xf*xf, axis=-1, keepdims=True) + EPS)
        h1 = ((xf*r)*gain_ref[0:1, :]).astype(bf16)
        c = cos_ref[:, t]; s = sin_ref[:, t]
        for w, dst, sc in ((0, qT_ref, 0.125), (1, kT_ref, 1.0)):
            y = tnt(wqkv_ref[w], h1)
            for h in range(H):
                a = y[h*HD:h*HD+32]; b = y[h*HD+32:h*HD+64]
                dst[h*HD:h*HD+32, t] = ((a*c - b*s)*sc).astype(bf16)
                dst[h*HD+32:h*HD+64, t] = ((b*c + a*s)*sc).astype(bf16)
        vT_ref[:, t] = tnt(wqkv_ref[2], h1).astype(bf16)
    for i in range(n):
        k0 = max(0, i-2)*B; nk = i*B + B - k0
        q0 = i*B
        kid = lax.broadcasted_iota(jnp.int32, (nk, B), 0) + k0
        qid = lax.broadcasted_iota(jnp.int32, (nk, B), 1) + q0
        ok = (segc_ref[k0:k0+nk, 0:1] == segr_ref[0:1, q0:q0+B]) & (kid <= qid)
        bias_s[0:nk, :] = jnp.where(ok, 0.0, NEG)
        @pl.loop(0, H//2)
        def _(p):
            for e in range(2):
                rows = pl.ds(pl.multiple_of(p*128 + e*64, 64), 64)
                s = tn(kT_ref[rows, k0:k0+nk], qT_ref[rows, q0:q0+B]) + bias_s[0:nk, :]
                m = jnp.max(s, axis=0, keepdims=True)
                ex = jnp.exp(s - m)
                l = jnp.sum(ex, axis=0, keepdims=True)
                o = nn(vT_ref[rows, k0:k0+nk], ex.astype(bf16)) * (1.0/l)
                oT_ref[rows, q0:q0+B] = o.astype(bf16)
                lse_ref[pl.ds(p*2+e, 1), q0:q0+B] = m + jnp.log(l)
        ob_ref[q0:q0+B, :] = oT_ref[:, q0:q0+B].T

def attn_fwd(lens, x, gains, freq, wqkv):
    S, D = x.shape
    sh = lambda s, d: jax.ShapeDtypeStruct(s, d)
    return pl.pallas_call(attn_fwd_body,
        in_specs=[pl.BlockSpec(memory_space=pltpu.SMEM)]+[VM]*4, out_specs=[VM]*10,
        out_shape=[sh((D,S),bf16), sh((D,S),bf16), sh((D,S),bf16), sh((S,D),bf16), sh((D,S),bf16), sh((16,S),f32),
                   sh((32,S),f32), sh((32,S),f32), sh((S,128),f32), sh((8,S),f32)],
        scratch_shapes=[pltpu.VMEM((768,256),f32)],
        compiler_params=pltpu.CompilerParams(vmem_limit_bytes=62*2**20), name="attn_fwd")(lens, x, gains, freq, wqkv)

def attn_bwd_body(x_ref, gain_ref, wqkv_ref, dmid_ref, qT_ref, kT_ref, vT_ref, dob_ref, dobT_ref, oT_ref, lse_ref, cos_ref, sin_ref, segc_ref, segr_ref,
                  ig_ref, dw_ref, bias_s, k_s, v_s, q_s, dqT_s, dk_s, dv_s, dkT_s, h1T_s, B=256):
    S, D = x_ref.shape
    n = S // B
    k_s[...] = kT_ref[...].T; v_s[...] = vT_ref[...].T; q_s[...] = qT_ref[...].T
    dk_s[...] = jnp.zeros_like(dk_s); dv_s[...] = jnp.zeros_like(dv_s)
    lane = lax.broadcasted_iota(jnp.int32, (B, 128), 1)
    for i in range(n):
        k0 = max(0, i-2)*B; nk = i*B + B - k0
        q0 = i*B
        kid = lax.broadcasted_iota(jnp.int32, (nk, B), 0) + k0
        qid = lax.broadcasted_iota(jnp.int32, (nk, B), 1) + q0
        ok = (segc_ref[k0:k0+nk, 0:1] == segr_ref[0:1, q0:q0+B]) & (kid <= qid)
        bias_s[0:nk, :] = jnp.where(ok, 0.0, NEG)
        @pl.loop(0, H//2)
        def _(p):
            cols = pl.ds(pl.multiple_of(p*128, 128), 128)
            dv = None
            for e in range(2):
                rows = pl.ds(pl.multiple_of(p*128 + e*64, 64), 64)
                mine = (lane < 64) if e == 0 else (lane >= 64)
                dobz = jnp.where(mine, dob_ref[q0:q0+B, cols], 0).astype(bf16)
                qz = jnp.where(mine, q_s[q0:q0+B, cols], 0).astype(bf16)
                s = tn(kT_ref[rows, k0:k0+nk], qT_ref[rows, q0:q0+B]) + bias_s[0:nk, :]
                pr = jnp.exp(s - lse_ref[pl.ds(p*2+e, 1), q0:q0+B])
                dp = tn(vT_ref[rows, k0:k0+nk], dobT_ref[rows, q0:q0+B])
                inner = jnp.sum(pr*dp, axis=0, keepdims=True)
                ds = (pr*(dp - inner)).astype(bf16)
                dve = nn(pr.astype(bf16), dobz)
                dke = nn(ds, qz)
                dqT_s[rows, q0:q0+B] = nn(kT_ref[rows, k0:k0+nk], ds) * 0.125
                dv = dve if dv is None else dv + dve
                dk = dke if e == 0 else dk + dke
            dv_s[k0:k0+nk, cols] += dv
            dk_s[k0:k0+nk, cols] += dk
    @pl.loop(0, n)
    def _(i):
        t = pl.ds(pl.multiple_of(i*B, B), B)
        c = cos_ref[:, t]; s = sin_ref[:, t]
        dkT = dk_s[t, :].T
        for src, dst in ((dqT_s[:, t], qT_ref), (dkT, kT_ref)):
            for h in range(H):
                a = src[h*HD:h*HD+32]; b = src[h*HD+32:h*HD+64]
                dqT_s[h*HD:h*HD+32, t] = a*c + b*s
                dqT_s[h*HD+32:h*HD+64, t] = b*c - a*s
            if dst is qT_ref:
                q_s[t, :] = dqT_s[:, t].astype(bf16).T
            else:
                k_s[t, :] = dqT_s[:, t].astype(bf16).T
        dvb = dv_s[t, :].astype(bf16)
        v_s[t, :] = dvb
        gain = gain_ref[0:1, :]
        xf = x_ref[t, :].astype(f32)
        r = lax.rsqrt(jnp.mean(xf*xf, axis=-1, keepdims=True) + EPS)
        xh = xf*r
        h1T_s[:, t] = (xh*gain).astype(bf16).T
        dh = nt(q_s[t, :], wqkv_ref[0]) + nt(k_s[t, :], wqkv_ref[1]) + nt(dvb, wqkv_ref[2])
        w = dh*gain
        ig_ref[t, :] = dmid_ref[t, :] + r*(w - xh*jnp.mean(w*xh, axis=-1, keepdims=True))
    dw_ref[0] = nn(h1T_s[...], q_s[...]).astype(bf16)
    dw_ref[1] = nn(h1T_s[...], k_s[...]).astype(bf16)
    dw_ref[2] = nn(h1T_s[...], v_s[...]).astype(bf16)

def attn_bwd(x, gains, wqkv, dmid, qT, kT, vT, dob, dobT, oT, lse, cos, sin, segc, segr):
    S, D = x.shape
    sh = lambda s, d: jax.ShapeDtypeStruct(s, d)
    return pl.pallas_call(attn_bwd_body,
        in_specs=[VM]*15, out_specs=[VM]*2,
        out_shape=[sh((S,D),f32), sh((3,D,D),bf16)],
        scratch_shapes=[pltpu.VMEM((768,256),f32), pltpu.VMEM((S,D),bf16), pltpu.VMEM((S,D),bf16), pltpu.VMEM((S,D),bf16),
                        pltpu.VMEM((D,S),f32), pltpu.VMEM((S,D),f32), pltpu.VMEM((S,D),f32), pltpu.VMEM((8,128),f32), pltpu.VMEM((D,S),bf16)],
        compiler_params=pltpu.CompilerParams(vmem_limit_bytes=62*2**20), name="attn_bwd")(x, gains, wqkv, dmid, qT, kT, vT, dob, dobT, oT, lse, cos, sin, segc, segr)


def adam_step(weight, grad_sum, moment, second, rate, decay):
    moment_new = beta_one * moment + (1.0 - beta_one) * grad_sum
    second_new = beta_two * second + (1.0 - beta_two) * grad_sum * grad_sum
    moment_hat = moment_new / (1.0 - beta_one**STEP)
    second_hat = second_new / (1.0 - beta_two**STEP)
    weight_new = weight - rate * (moment_hat / (jnp.sqrt(second_hat) + adam_eps) + decay * weight)
    return (moment_new, second_new, weight_new)


def per_device(tokens, seg_lens, cotangent, qkv_w, out_w, gu_w, down_w, gains,
               qkv_m, qkv_v, out_m, out_v, gu_m, gu_v, down_m, down_v, gain_m, gain_v):
    _, S, D = tokens.shape
    x = tokens.reshape(S, D)
    cot = cotangent.reshape(S, D)
    gain_low = gains.astype(bf16)
    wqkv = lax.all_gather(qkv_w.astype(bf16), "dp", axis=1, tiled=True)
    gain_full = lax.all_gather(gain_low, "dp", axis=1, tiled=True).astype(f32)
    wo = lax.all_gather(out_w.astype(bf16), "dp", axis=0, tiled=True)
    wgu = lax.all_gather(gu_w.astype(bf16), "dp", axis=1, tiled=True)
    wd = lax.all_gather(down_w.astype(bf16), "dp", axis=0, tiled=True)
    gain8 = jnp.pad(gain_full, ((0, 6), (0, 0)))
    freq = 10000.0 ** (-jnp.arange(HD // 2, dtype=f32) / (HD // 2))
    freq = jnp.broadcast_to(freq[:, None], (HD // 2, 128))
    qT, kT, vT, ob, oT, lse, cos, sin, segc, segr = attn_fwd(seg_lens, x, gain8, freq, wqkv)
    output, dmid, dob, dobT, dwo, dwgu, dwd = mlp(x, ob, oT, cot, wo, wgu, wd, gain8)
    input_grad, dwqkv = attn_bwd(x, gain8, wqkv, dmid, qT, kT, vT, dob, dobT, oT, lse, cos, sin, segc, segr)

    def owned(grad, axis):
        part = lax.psum_scatter(grad, "dp", scatter_dimension=axis, tiled=True)
        return lax.psum(part.astype(f32), "rep")

    g_down = owned(dwd, 0)
    g_gu = owned(dwgu, 1)
    g_out = owned(dwo, 0)
    g_qkv = owned(dwqkv, 1)
    gain_f = gain_low.astype(f32)
    g_gain = jnp.stack([
        jnp.sum(g_qkv * qkv_w.astype(bf16).astype(f32), axis=(0, 2)) / gain_f[0],
        jnp.sum(g_gu * gu_w.astype(bf16).astype(f32), axis=(0, 2)) / gain_f[1],
    ])
    qkv_res = adam_step(qkv_w, g_qkv, qkv_m, qkv_v, matrix_rate, weight_decay)
    out_res = adam_step(out_w, g_out, out_m, out_v, matrix_rate, weight_decay)
    gu_res = adam_step(gu_w, g_gu, gu_m, gu_v, matrix_rate, weight_decay)
    down_res = adam_step(down_w, g_down, down_m, down_v, matrix_rate, weight_decay)
    gain_res = adam_step(gains, g_gain, gain_m, gain_v, gain_rate, 0.0)
    return (output.reshape(tokens.shape), input_grad.reshape(tokens.shape)) + qkv_res + out_res + gu_res + down_res + gain_res


def solution(mesh):
    rows, cols, vec = P(("dp", "rep"), None, None), P(None, "dp", None), P("dp", None)
    small = P(None, "dp")
    return jax.shard_map(
        per_device,
        mesh=mesh,
        in_specs=(rows, P(("dp", "rep"), None), rows, cols, vec, cols, vec, small,
                  cols, cols, vec, vec, cols, cols, vec, vec, small, small),
        out_specs=(rows, rows) + (cols,) * 3 + (vec,) * 3 + (cols,) * 3 + (vec,) * 3 + (small,) * 3,
        check_vma=False,
    )
```

time: 755 us -> 558 us (0.74); the launches traced: 745 us -> 558 us
  matrix products: 255 us -> 0 us
  Pallas kernels: 0 us -> 140 us
  other arithmetic: 109 us -> 16.5 us
  local copies, waits for them, and re-layouts: 67.7 us -> 2.23 us
  blocking collectives: 71 us -> 136 us
  waiting for transfers between devices: 226 us -> 248 us
    dot_general x24 -> x0, matrix products: 255 us -> none  [the longest x2 40.4 us: attend_backward(): jnp.einsum('qhd,khd->hqk', grad_blk, value_row, preferred_element_type=jn...]
    pallas_call x0 -> x3, Pallas kernels: none -> 140 us  [the longest x1 52.1 us: attn_bwd(): pl.pallas_call(attn_bwd_body, in_specs=[VM] * 15, out_specs=[VM] * 2, out...]
    all_gather x4, waiting for transfers between devices: 22.7 us -> 96.6 us  [the longest x1 47.9 us: per_device(): wgu = lax.all_gather(gu_w.astype(bf16), 'dp', axis=1, tiled=True)]
    psum x1 -> x0, waiting for transfers between devices: 67.5 us -> none  [per_device(): lax.psum((sum_qkv, sum_out, sum_gain, sum_gu, sum_down), 'rep')]
    psum x1, blocking collectives: 60.8 us -> 126 us  [owned(): return lax.psum(part.astype(f32), 'rep')]
    reduce_scatter x2 -> x4, waiting for transfers between devices: 92.9 us -> 150 us  [owned(): part = lax.psum_scatter(grad, 'dp', scatter_dimension=axis, tiled=True)]
    convert_element_type x7 -> x5, other arithmetic: 50.5 us -> 4.51 us  [the longest x1 2.05 us: per_device(): wqkv = lax.all_gather(qkv_w.astype(bf16), 'dp', axis=1, tiled=True)]
    unnamed x138 -> x31, local copies, waits for them, and re-layouts: 43.8 us -> 1.55 us
  transfers between devices with their start and end apart: 10 -> 8, of which waited for: 7 -> 6; matrix products, arithmetic and copies ran while one was open for 44% -> 1% of each run, Pallas kernels for 0% -> 16%
where the time goes in v1:
time: 558 us
  waiting for transfers between devices  248 us (44%)
  Pallas kernels  140 us (25%)
  blocking collectives  136 us (24%)
  other arithmetic  16.5 us (3%)
  between operations  14.4 us (3%)
    reduce_scatter x4, waiting for transfers between devices, owned(): part = lax.psum_scatter(grad, 'dp', scatter_dimension=axis, tiled=True)  150 us
    psum x1, blocking collectives, owned(): return lax.psum(part.astype(f32), 'rep')  126 us
    pallas_call x1, Pallas kernels, attn_bwd(): pl.pallas_call(attn_bwd_body, in_specs=[VM] * 15, out_specs=[VM] * 2, out...  52.1 us
    pallas_call x1, Pallas kernels, mlp(): pl.pallas_call(functools.partial(mlp_kernel, T), grid=(FF // FC,), in_spe...  51.9 us
    all_gather x1, waiting for transfers between devices, per_device(): wgu = lax.all_gather(gu_w.astype(bf16), 'dp', axis=1, tiled=True)  47.9 us
    pallas_call x1, Pallas kernels, attn_fwd(): pl.pallas_call(attn_fwd_body, in_specs=[pl.BlockSpec(memory_space=pltpu.S...  36.2 us
    all_gather x1, waiting for transfers between devices, per_device(): wd = lax.all_gather(down_w.astype(bf16), 'dp', axis=0, tiled=True)  24.6 us
    all_gather x1, waiting for transfers between devices, per_device(): wqkv = lax.all_gather(qkv_w.astype(bf16), 'dp', axis=1, tiled=True)  24.2 us
  transfers between devices with their start and end apart: 8, of which 6 were waited for; matrix products, arithmetic and copies ran while one was open for 1% of the time, Pallas kernels for 16%

profile of v1, /device:TPU:0, one launch (start us, length us, event | category | flops | bytes accessed | tf_op | source)
XLA Modules:
  0.0 557.7 jit_solution(17519769017815906838)
XLA Ops:
  7.3 2.1 convert_element_type.42
  9.3 0.0 all-gather.8.cloned.1.call-start
  9.4 0.7 convert_element_type.43
  10.1 0.0 all-gather.12.cloned.1.call-start
  10.2 0.8 convert_element_type.45
  11.0 1.0 convert_element_type.44
  12.1 0.0 reduce-scatter.7.cloned.1.call-start
  12.1 10.2 %all-gather = bf16[8,96,2]{1,2,0:T(2,128)(2,1)S(1)} all-gather(bf16[1,96,2]{1,2,0:T(2,128)(2,1)S(1)} %get-tuple-element.79), channel_id=1, replica_groups=mesh['dp'=8,'rep'=4] {'dp'}, dimensions={0}, use_global_device_ids=true | all-gather | bytes 3456 | tf_op jit(solution)/shard_map/all_gather | solution.py:250
  22.3 0.1 reshape.59
  22.4 0.6 pad_convert_fusion.gain_ref
  23.1 24.2 %all-gather.6.cloned.1.call-done.wqkv_ref = bf16[3,768,768]{2,1,0:T(8,128)(2,1)} async-done(((bf16[3,96,768]{2,1,0:T(8,128)(2,1)}), bf16[3,768,768]{2,1,0:T(8,128)(2,1)}) %all-gather.6.cloned.1.call-update) | async-done | bytes 3538960 | tf_op jit(solution)/shard_map/all_gather | solution.py:249
  47.2 0.7 broadcast_in_dim.2.freq_ref
  47.9 36.2 %attn_fwd.1 = (bf16[768,1024]{1,0:T(8,128)(2,1)}, bf16[768,1024]{1,0:T(8,128)(2,1)}, bf16[768,1024]{1,0:T(8,128)(2,1)}, bf16[1024,768]{1,0:T(8,128)(2,1)}, bf16[...) custom-call(s32[1,5]{1,0:T(1,128)} %lens_ref.1, ...), custom_call_target="tpu_custom_call" | custom-call | tf_op jit(solution)/shard_map/attn_fwd/pallas_call | solution.py:153
  84.2 24.6 %all-gather.12.cloned.1.call-done.wd_ref = bf16[2048,768]{1,0:T(8,128)(2,1)} async-done(((bf16[256,768]{1,0:T(8,128)(2,1)}), bf16[2048,768]{1,0:T(8,128)(2,1)}) %all-gather.12.cloned.1.call-update) | async-done | bytes 3145744 | tf_op jit(solution)/shard_map/all_gather | solution.py:253
  108.7 47.9 %all-gather.10.cloned.1.call-done.wgu_ref = bf16[2,768,2048]{2,1,0:T(8,128)(2,1)} async-done(((bf16[2,96,2048]{2,1,0:T(8,128)(2,1)}), bf16[2,768,2048]{2,1,0:T(8,128)(2,1)}) %all-gather.10.cloned.1.call-update) | async-done | bytes 6291472 | tf_op jit(solution)/shard_map/all_gather | solution.py:252
  156.6 51.9 %mlp.1 = (f32[1024,768]{1,0:T(8,128)}, f32[1024,768]{1,0:T(8,128)}, bf16[1024,768]{1,0:T(8,128)(2,1)}, bf16[768,1024]{1,0:T(8,128)(2,1)}, bf16[768,768]{1,0:T(8,...) custom-call(bf16[1024,768]{1,0:T(8,128)(2,1)} %bitcast.16, ...), custom_call_target="tpu_custom_call" | custom-call | tf_op jit(solution)/shard_map/mlp/pallas_call | solution.py:76
  208.6 0.5 reduce-scatter.11.cloned.1.call-update
  209.2 0.2 reduce-scatter.5.cloned.1.call-start
  209.4 52.1 %attn_bwd.1 = (f32[1024,768]{1,0:T(8,128)}, bf16[3,768,768]{2,1,0:T(8,128)(2,1)}) custom-call(bf16[1024,768]{1,0:T(8,128)(2,1)} %bitcast.17, f32[8,768]{1,0:T(8,128)} %pad_convert_fusion.gain_ref, bf16[3,768,768]{2,1,0:T(8,128)(2,1)} %all-gather.6.cloned.1.call-done.wqkv_ref, f32[1024,768]{1,0:T(8,128)} %get-tuple-element.39.dmid_ref, ...), custom_call_target="tpu_custom_call" | custom-call | tf_op jit(solution)/shard_map/attn_bwd/pallas_call | solution.py:226
  261.5 0.0 reduce-scatter.9.cloned.1.call-start
  261.5 0.7 reduce-scatter.9.cloned.1.call-update
  262.3 33.1 %reduce-scatter.11.cloned.1.call-done = bf16[256,768]{1,0:T(8,128)(2,1)} async-done(((bf16[2048,768]{1,0:T(8,128)(2,1)}), bf16[256,768]{1,0:T(8,128)(2,1)}) %reduce-scatter.11.cloned.1.call-update) | async-done | bytes 393232 | tf_op jit(solution)/shard_map/reduce_scatter | solution.py:262
  295.4 51.6 %reduce-scatter.5.cloned.1.call-done = bf16[3,96,768]{2,1,0:T(8,128)(2,1)} async-done(((bf16[3,768,768]{2,1,0:T(8,128)(2,1)}), bf16[3,96,768]{2,1,0:T(8,128)(2,1)}) %reduce-scatter.5.cloned.1.call-update) | async-done | bytes 442384 | tf_op jit(solution)/shard_map/reduce_scatter | solution.py:262
  347.0 65.2 %reduce-scatter.9.cloned.1.call-done = bf16[2,96,2048]{2,1,0:T(8,128)(2,1)} async-done(((bf16[2,768,2048]{2,1,0:T(8,128)(2,1)}), bf16[2,96,2048]{2,1,0:T(8,128)(2,1)}) %reduce-scatter.9.cloned.1.call-update) | async-done | bytes 786448 | tf_op jit(solution)/shard_map/reduce_scatter | solution.py:262
  412.2 125.8 %all-reduce.3 = (f32[3,96,768]{2,1,0:T(8,128)}, f32[96,768]{1,0:T(8,128)}, f32[2,96,2048]{2,1,0:T(8,128)}, f32[256,768]{1,0:T(8,128)S(1)}) all-reduce(bf16[3,96,768]{2,1,0:T(8,128)(2,1)} %reduce-scatter.5.cloned.1.call-done, bf16[96,768]{1,0:T(8,128)(2,1)} %reduce-scatter.7.cloned.1.call-done, ...), channel_id=1, replica_groups=mesh['dp'=8,'rep'=4] {'rep'}, use_global_device_ids=true, to_apply=%region_1.2 | all-reduce | flops 884736 | bytes 5308416 | tf_op jit(solution)/shard_map/psum | solution.py:263
  537.9 2.3 multiply_subtract_fusion.3
  540.3 3.4 multiply_subtract_fusion.1
  543.8 1.8 multiply_subtract_fusion.2
  545.6 0.9 copy-done.5
  546.5 0.5 copy-done.6
  547.0 3.2 multiply_subtract_fusion
  550.2 0.6 multiply_subtract_fusion.4
  (43 shorter events, 0.4 us)
Async XLA Ops:
  7.2 2.2 copy-start.7
  7.2 3.0 copy-start.2
  7.2 40.0 %all-gather.6.cloned.1.call-start = ((), (), s32[]{:S(2)}) async-start(), calls=%async_computation.4 | async-start | bytes 3981312 | tf_op jit(solution)/shard_map/all_gather | solution.py:249
  9.3 1.7 copy-start
  9.3 74.8 %all-gather.8.cloned.1.call-start = ((), (), s32[]{:S(2)}) async-start(), calls=%async_computation.5 | async-start | bytes 1327104 | tf_op jit(solution)/shard_map/all_gather | solution.py:251
  10.1 98.6 %all-gather.12.cloned.1.call-start = ((), (), s32[]{:S(2)}) async-start(), calls=%async_computation.7 | async-start | bytes 3538944 | tf_op jit(solution)/shard_map/all_gather | solution.py:253
  11.0 1.1 copy-start.12
  11.0 145.7 %all-gather.10.cloned.1.call-start = ((), (), s32[]{:S(2)}) async-start(), calls=%async_computation.6 | async-start | bytes 7077888 | tf_op jit(solution)/shard_map/all_gather | solution.py:252
  12.1 250.2 %reduce-scatter.7.cloned.1.call-start = ((), (), s32[]{:S(2)}) async-start(), calls=%async_computation.9 | async-start | bytes 1327104 | tf_op jit(solution)/shard_map/reduce_scatter | solution.py:262
  208.6 86.8 %reduce-scatter.11.cloned.1.call-start = ((), (), s32[]{:S(2)}) async-start(), calls=%async_computation.11 | async-start | bytes 3538944 | tf_op jit(solution)/shard_map/reduce_scatter | solution.py:262
  209.2 137.9 %reduce-scatter.5.cloned.1.call-start = ((), (), s32[]{:S(2)}) async-start(), calls=%async_computation.8 | async-start | bytes 3981312 | tf_op jit(solution)/shard_map/reduce_scatter | solution.py:262
  261.5 150.7 %reduce-scatter.9.cloned.1.call-start = ((), (), s32[]{:S(2)}) async-start(), calls=%async_computation.10 | async-start | bytes 7077888 | tf_op jit(solution)/shard_map/reduce_scatter | solution.py:262
  262.2 278.0 %copy-start.1 = (f32[3,96,768]{2,1,0:T(8,128)S(1)}, f32[3,96,768]{2,1,0:T(8,128)}, u32[]{:S(2)}) copy-start(f32[3,96,768]{2,1,0:T(8,128)} %param.21) | copy-start | bytes 2654212
  537.9 2.3 copy-start.8
  537.9 2.3 copy-start.9
  540.3 3.5 copy-start.3
  540.3 3.5 copy-start.10
  540.3 3.5 copy-start.11
  543.7 1.8 copy-start.4
  543.8 2.7 copy-start.5
  543.8 3.2 copy-start.6
  547.0 3.2 copy-start.13
  547.0 3.2 copy-start.14
Sparse Core Ops, SparseCore 0:
  10.5 36.6 all-gather.5
  49.7 24.0 all-gather.7
  76.3 32.4 all-gather.11
  111.1 45.5 all-gather.9
  208.7 36.7 reduce-scatter.6
  249.1 46.2 reduce-scatter.10
  298.9 48.0 reduce-scatter.4
  350.4 61.7 reduce-scatter.8

commit v2 on v1

--- a/solution.py
+++ b/solution.py
@@ -87,6 +87,7 @@
         compiler_params=pltpu.CompilerParams(vmem_limit_bytes=62*2**20),
         name="mlp",
     )(x, ob, obT, cot, wo, wgu, wd, gains)
+
 H, HD = 12, 64
 NEG = -1e30
 VM = pl.BlockSpec(memory_space=pltpu.VMEM)
@@ -102,60 +103,6 @@
         seg += past
         start += past * lens_ref[0, s]
     return seg, slot - start
-
-def attn_fwd_body(lens_ref, x_ref, gain_ref, freq_ref, wqkv_ref, qT_ref, kT_ref, vT_ref, ob_ref, oT_ref, lse_ref, cos_ref, sin_ref, segc_ref, segr_ref,
-                 bias_s, B=256):
-    S, D = x_ref.shape
-    n = S // B
-    seg, place = seg_rows(lens_ref, S)
-    ang = jnp.broadcast_to(place[0:1, :].astype(f32), (HD//2, S)) * freq_ref[:, 0:1]
-    cos_ref[...] = jnp.cos(ang); sin_ref[...] = jnp.sin(ang)
-    segf = jnp.broadcast_to(seg[0:1, :].astype(f32), (128, S))
-    segr_ref[...] = segf[0:8]
-    segc_ref[...] = segf.T
-    @pl.loop(0, n)
-    def _(i):
-        t = pl.ds(pl.multiple_of(i*B, B), B)
-        xf = x_ref[t, :].astype(f32)
-        r = lax.rsqrt(jnp.mean(xf*xf, axis=-1, keepdims=True) + EPS)
-        h1 = ((xf*r)*gain_ref[0:1, :]).astype(bf16)
-        c = cos_ref[:, t]; s = sin_ref[:, t]
-        for w, dst, sc in ((0, qT_ref, 0.125), (1, kT_ref, 1.0)):
-            y = tnt(wqkv_ref[w], h1)
-            for h in range(H):
-                a = y[h*HD:h*HD+32]; b = y[h*HD+32:h*HD+64]
-                dst[h*HD:h*HD+32, t] = ((a*c - b*s)*sc).astype(bf16)
-                dst[h*HD+32:h*HD+64, t] = ((b*c + a*s)*sc).astype(bf16)
-        vT_ref[:, t] = tnt(wqkv_ref[2], h1).astype(bf16)
-    for i in range(n):
-        k0 = max(0, i-2)*B; nk = i*B + B - k0
-        q0 = i*B
-        kid = lax.broadcasted_iota(jnp.int32, (nk, B), 0) + k0
-        qid = lax.broadcasted_iota(jnp.int32, (nk, B), 1) + q0
-        ok = (segc_ref[k0:k0+nk, 0:1] == segr_ref[0:1, q0:q0+B]) & (kid <= qid)
-        bias_s[0:nk, :] = jnp.where(ok, 0.0, NEG)
-        @pl.loop(0, H//2)
-        def _(p):
-            for e in range(2):
-                rows = pl.ds(pl.multiple_of(p*128 + e*64, 64), 64)
-                s = tn(kT_ref[rows, k0:k0+nk], qT_ref[rows, q0:q0+B]) + bias_s[0:nk, :]
-                m = jnp.max(s, axis=0, keepdims=True)
-                ex = jnp.exp(s - m)
-                l = jnp.sum(ex, axis=0, keepdims=True)
-                o = nn(vT_ref[rows, k0:k0+nk], ex.astype(bf16)) * (1.0/l)
-                oT_ref[rows, q0:q0+B] = o.astype(bf16)
-                lse_ref[pl.ds(p*2+e, 1), q0:q0+B] = m + jnp.log(l)
-        ob_ref[q0:q0+B, :] = oT_ref[:, q0:q0+B].T
-
-def attn_fwd(lens, x, gains, freq, wqkv):
-    S, D = x.shape
-    sh = lambda s, d: jax.ShapeDtypeStruct(s, d)
-    return pl.pallas_call(attn_fwd_body,
-        in_specs=[pl.BlockSpec(memory_space=pltpu.SMEM)]+[VM]*4, out_specs=[VM]*10,
-        out_shape=[sh((D,S),bf16), sh((D,S),bf16), sh((D,S),bf16), sh((S,D),bf16), sh((D,S),bf16), sh((16,S),f32),
-                   sh((32,S),f32), sh((32,S),f32), sh((S,128),f32), sh((8,S),f32)],
-        scratch_shapes=[pltpu.VMEM((768,256),f32)],
-        compiler_params=pltpu.CompilerParams(vmem_limit_bytes=62*2**20), name="attn_fwd")(lens, x, gains, freq, wqkv)
 
 def attn_bwd_body(x_ref, gain_ref, wqkv_ref, dmid_ref, qT_ref, kT_ref, vT_ref, dob_ref, dobT_ref, oT_ref, lse_ref, cos_ref, sin_ref, segc_ref, segr_ref,
                   ig_ref, dw_ref, bias_s, k_s, v_s, q_s, dqT_s, dk_s, dv_s, dkT_s, h1T_s, B=256):
@@ -230,6 +177,210 @@
                         pltpu.VMEM((D,S),f32), pltpu.VMEM((S,D),f32), pltpu.VMEM((S,D),f32), pltpu.VMEM((8,128),f32), pltpu.VMEM((D,S),bf16)],
         compiler_params=pltpu.CompilerParams(vmem_limit_bytes=62*2**20), name="attn_bwd")(x, gains, wqkv, dmid, qT, kT, vT, dob, dobT, oT, lse, cos, sin, segc, segr)
 
+MESH = pl.DeviceIdType.MESH
+
+def flip(v, b):
+    return v + b - 2*b*lax.rem(lax.div(v, b), 2)
+
+def places():
+    d = lax.axis_index("dp"); z = lax.axis_index("rep")
+    sib, xn, yn = flip(d, 1), flip(d, 2), flip(d, 4)
+    xy = flip(xn, 4)
+    return d, z, sib, xn, yn, xy
+
+def greet(devs):
+    bar = pltpu.get_barrier_semaphore()
+    for dev in devs:
+        pl.semaphore_signal(bar, inc=1, device_id=dev, device_id_type=MESH)
+    pl.semaphore_wait(bar, len(devs))
+
+class Gather:
+    N = 15
+    def __init__(self, ref, view, send, recv, g):
+        self.ref, self.view, self.send, self.recv, self.g = ref, view, send, recv, g
+        d, z, sib, xn, yn, xy = places()
+        zn = flip(z, 1)
+        S, X, Y, Z = (sib, z), (xn, z), (yn, z), (d, zn)
+        self.moves = [(d, "all", S), (d, "zb", X), (d, "zb", Y),
+                      (xn, "zb", S), (xn, "z", Y), (xn, "z", Z),
+                      (yn, "zb", S), (yn, "b", X), (yn, "z", Z),
+                      (xy, "z", S), (xy, "z", Z), (xy, "b", S),
+                      (xn, "o", S), (yn, "o", S), (xy, "o", S)]
+        self.after = {1: (3, 4, 5), 2: (6, 7, 8), 4: (9, 10), 7: (11,), 5: (12,), 8: (13,), 10: (14,)}
+    def copy(self, k):
+        d, part, dev = self.moves[k]
+        v = self.view(self.ref, d, part)
+        return pltpu.make_async_remote_copy(src_ref=v, dst_ref=v, send_sem=self.send.at[self.g, k], recv_sem=self.recv.at[self.g, k],
+                                            device_id=dev, device_id_type=MESH)
+    def begin(self):
+        for k in (1, 2, 0): self.copy(k).start()
+    def got(self, *ks):
+        for k in ks:
+            self.copy(k).wait_recv()
+            for j in self.after.get(k, ()): self.copy(j).start()
+    def first(self): self.got(1, 2)
+    def second(self): self.got(4, 7, 5, 8)
+    def third(self): self.got(10)
+    def sibling(self): self.got(0, 3, 6, 9, 11, 12, 13, 14)
+    def sent(self):
+        for k in range(self.N): self.copy(k).wait_send()
+
+def row_view(rows, a, lead):
+    z = lax.axis_index("rep"); p = lax.rem(z, 2)
+    def view(ref, d, part):
+        off, n = {"all": (0, rows), "zb": (p*a, rows - a), "z": (p*(rows - a), a), "b": (a, rows - 2*a), "o": ((1 - p)*(rows - a), a)}[part]
+        s = pl.ds(pl.multiple_of(d*rows + off, 16), n)
+        return ref.at[:, s, :] if lead else ref.at[s, :]
+    return view
+
+def cut(rows):
+    return rows // 3 // 16 * 16
+
+def can_gather(mesh_dp, mesh_rep, *rows):
+    return mesh_dp == 8 and mesh_rep % 2 == 0 and all(r % 16 == 0 and cut(r) > 0 for r in rows)
+
+ANY = pl.BlockSpec(memory_space=pl.ANY)
+SM = pl.BlockSpec(memory_space=pltpu.SMEM)
+B = 256
+
+def spread_gain(pieces, D):
+    n, wide = pieces.shape[0], D // pieces.shape[0]
+    r = lax.broadcasted_iota(jnp.int32, (n*128, D), 0); c = lax.broadcasted_iota(jnp.int32, (n*128, D), 1)
+    pick = (c == lax.div(r, 128)*wide + lax.rem(r, 128)) & (lax.rem(r, 128) < wide)
+    flat = jnp.concatenate([pieces[i] for i in range(n)], axis=1).astype(bf16)
+    return nn(flat, jnp.where(pick, 1.0, 0.0).astype(bf16))
+
+def forward_attention(lens_ref, x_ref, freq_ref, gain_of, weights_in, w_ref, qT_s, kT_s, vT_s, oT_s, lse_s, cos_s, sin_s, segc_s, segr_s, bias_s, hook):
+    S, D = x_ref.shape
+    n = S // B
+    seg, place = seg_rows(lens_ref, S)
+    ang = jnp.broadcast_to(place[0:1, :].astype(f32), (HD//2, S)) * freq_ref[:, 0:1]
+    cos_s[...] = jnp.cos(ang); sin_s[...] = jnp.sin(ang)
+    segf = jnp.broadcast_to(seg[0:1, :].astype(f32), (128, S))
+    segr_s[...] = segf[0:8]
+    segc_s[...] = segf.T
+    weights_in()
+    gain = gain_of()
+    @pl.loop(0, n)
+    def _(i):
+        t = pl.ds(pl.multiple_of(i*B, B), B)
+        xf = x_ref[t, :].astype(f32)
+        r = lax.rsqrt(jnp.mean(xf*xf, axis=-1, keepdims=True) + EPS)
+        h1 = ((xf*r)*gain).astype(bf16)
+        c = cos_s[:, t]; s = sin_s[:, t]
+        for w, dst, sc in ((0, qT_s, 0.125), (1, kT_s, 1.0)):
+            y = tnt(w_ref[w], h1)
+            for h in range(H):
+                a = y[h*HD:h*HD+32]; b = y[h*HD+32:h*HD+64]
+                dst[h*HD:h*HD+32, t] = ((a*c - b*s)*sc).astype(bf16)
+                dst[h*HD+32:h*HD+64, t] = ((b*c + a*s)*sc).astype(bf16)
+        vT_s[:, t] = tnt(w_ref[2], h1).astype(bf16)
+    hook("proj")
+    for i in range(n):
+        k0 = max(0, i-2)*B; nk = i*B + B - k0
+        q0 = i*B
+        kid = lax.broadcasted_iota(jnp.int32, (nk, B), 0) + k0
+        qid = lax.broadcasted_iota(jnp.int32, (nk, B), 1) + q0
+        ok = (segc_s[k0:k0+nk, 0:1] == segr_s[0:1, q0:q0+B]) & (kid <= qid)
+        bias_s[0:nk, :] = jnp.where(ok, 0.0, NEG)
+        @pl.loop(0, H//2)
+        def _(p):
+            for e in range(2):
+                rows = pl.ds(pl.multiple_of(p*128 + e*64, 64), 64)
+                s = tn(kT_s[rows, k0:k0+nk], qT_s[rows, q0:q0+B]) + bias_s[0:nk, :]
+                m = jnp.max(s, axis=0, keepdims=True)
+                ex = jnp.exp(s - m)
+                l = jnp.sum(ex, axis=0, keepdims=True)
+                o = nn(vT_s[rows, k0:k0+nk], ex.astype(bf16)) * (1.0/l)
+                oT_s[rows, q0:q0+B] = o.astype(bf16)
+                lse_s[pl.ds(p*2+e, 1), q0:q0+B] = m + jnp.log(l)
+        hook(i)
+
+def ka_body(sizes, lens_ref, x_ref, freq_ref, gain_ref, qw_ref, ow_ref, gw_ref, dw_ref,
+            qT_o, kT_o, vT_o, oT_o, lse_ref, cos_ref, sin_ref, segc_ref, segr_ref, gain8_ref, wq_o, wo_o, wgu_o, wd_o,
+            qT_s, kT_s, vT_s, oT_s, bias_s, wq_s, ost_s, gst_s, dst_s, of_s, gf_s, df_s, gp_s, send, recv, gsend, grecv, loc):
+    n_dp, n_rep = sizes
+    D = x_ref.shape[1]
+    d, z, sib, xn, yn, xy = places()
+    others = [lax.rem(d + j, n_dp) for j in range(1, n_dp)]
+    loads = [pltpu.make_async_copy(a, b, loc.at[i]) for i, (a, b) in enumerate(((ow_ref, of_s), (gw_ref, gf_s), (dw_ref, df_s)))]
+    for c in loads: c.start()
+    gp_s[pl.ds(d, 1)] = gain_ref[...].reshape(1, 8, 128)
+    rq, ro, rg, rd = qw_ref.shape[1], ow_ref.shape[0], gw_ref.shape[1], dw_ref.shape[0]
+    G = [Gather(full, row_view(r, cut(r), ld), send, recv, g)
+         for g, (full, r, ld) in enumerate(((wq_s, rq, True), (wo_o, ro, False), (wgu_o, rg, True), (wd_o, rd, False)))]
+    wq_s[:, pl.ds(pl.multiple_of(d*rq, 16), rq), :] = qw_ref[...].astype(bf16)
+    greet([(o, z) for o in others] + [(d, flip(z, 1))])
+    gains = [pltpu.make_async_remote_copy(src_ref=gp_s.at[d], dst_ref=gp_s.at[d], send_sem=gsend.at[j], recv_sem=grecv.at[j],
+                                          device_id=(o, z), device_id_type=MESH) for j, o in enumerate(others)]
+    for c in gains: c.start()
+    G[0].begin()
+    stage = []
+    for i, (f_s, b_s) in enumerate(((of_s, ost_s), (gf_s, gst_s), (df_s, dst_s))):
+        loads[i].wait()
+        b_s[...] = f_s[...].astype(bf16)
+        g = G[i+1]
+        c = pltpu.make_async_copy(b_s, g.view(g.ref, d, "all"), loc.at[3+i]); c.start()
+        stage.append(c)
+    outs = []
+    def out(src, dst):
+        c = pltpu.make_async_copy(src, dst, loc.at[6 + len(outs)]); c.start(); outs.append(c)
+    def weights_in():
+        G[0].first()
+        for i in range(3):
+            stage[i].wait(); G[1+i].begin()
+        G[0].second(); G[0].third(); G[0].sibling()
+        out(wq_s, wq_o)
+    def gain_of():
+        for c in gains: c.wait_recv()
+        full = spread_gain(gp_s[...], D)
+        gain8_ref[...] = full
+        return full[0:1, :]
+    def hook(at):
+        if at == "proj":
+            out(qT_s, qT_o); out(kT_s, kT_o); out(vT_s, vT_o)
+        elif at == 1:
+            G[1].first(); G[2].first()
+        elif at == 2:
+            G[3].first(); G[1].second(); G[1].third(); G[2].second()
+        elif at == 3:
+            out(oT_s, oT_o)
+            G[2].third(); G[3].second(); G[3].third()
+            for g in G[1:]: g.sibling()
+    forward_attention(lens_ref, x_ref, freq_ref, gain_of, weights_in, wq_s, qT_s, kT_s, vT_s, oT_s, lse_ref, cos_ref, sin_ref, segc_ref, segr_ref, bias_s, hook)
+    for c in gains: c.wait_send()
+    for g in G: g.sent()
+    for c in outs: c.wait()
+
+def ka(n_dp, n_rep, lens, x, freq, gain_piece, qw, ow, gw, dw):
+    S, D = x.shape
+    FF = gw.shape[2]
+    sh = lambda s, d: jax.ShapeDtypeStruct(s, d)
+    return pl.pallas_call(functools.partial(ka_body, (n_dp, n_rep)),
+        in_specs=[SM, VM, VM, VM, VM, ANY, ANY, ANY], out_specs=[ANY]*4+[VM]*6+[ANY]*4,
+        out_shape=[sh((D,S),bf16)]*4 + [sh((16,S),f32), sh((32,S),f32), sh((32,S),f32), sh((S,128),f32), sh((8,S),f32), sh((8,D),f32),
+                   sh((3,D,D),bf16), sh((D,D),bf16), sh((2,D,FF),bf16), sh((FF,D),bf16)],
+        scratch_shapes=[pltpu.VMEM((D,S),bf16)]*4 + [pltpu.VMEM((768,256),f32), pltpu.VMEM((3,D,D),bf16),
+                        pltpu.VMEM(ow.shape,bf16), pltpu.VMEM(gw.shape,bf16), pltpu.VMEM(dw.shape,bf16),
+                        pltpu.VMEM(ow.shape,f32), pltpu.VMEM(gw.shape,f32), pltpu.VMEM(dw.shape,f32), pltpu.VMEM((n_dp,8,128),f32),
+                        pltpu.SemaphoreType.DMA((4,15)), pltpu.SemaphoreType.DMA((4,15)), pltpu.SemaphoreType.DMA((n_dp-1,)), pltpu.SemaphoreType.DMA((n_dp-1,)),
+                        pltpu.SemaphoreType.DMA((16,))],
+        compiler_params=pltpu.CompilerParams(collective_id=0, has_side_effects=True, vmem_limit_bytes=62*2**20),
+        cost_estimate=pl.CostEstimate(flops=12*10**9, bytes_accessed=30*10**6, transcendentals=7*10**6),
+        name="gather_attend")(lens, x, freq, gain_piece, qw, ow, gw, dw)
+
+def local_body(lens_ref, x_ref, freq_ref, gain_ref, w_ref, qT_ref, kT_ref, vT_ref, oT_ref, lse_ref, cos_ref, sin_ref, segc_ref, segr_ref, bias_s):
+    forward_attention(lens_ref, x_ref, freq_ref, lambda: gain_ref[0:1, :], lambda: None, w_ref, qT_ref, kT_ref, vT_ref, oT_ref,
+                      lse_ref, cos_ref, sin_ref, segc_ref, segr_ref, bias_s, lambda at: None)
+
+def attn_fwd(lens, x, gains, freq, wqkv):
+    S, D = x.shape
+    sh = lambda s, d: jax.ShapeDtypeStruct(s, d)
+    return pl.pallas_call(local_body,
+        in_specs=[SM]+[VM]*4, out_specs=[VM]*9,
+        out_shape=[sh((D,S),bf16)]*4 + [sh((16,S),f32), sh((32,S),f32), sh((32,S),f32), sh((S,128),f32), sh((8,S),f32)],
+        scratch_shapes=[pltpu.VMEM((768,256),f32)],
+        compiler_params=pltpu.CompilerParams(vmem_limit_bytes=62*2**20), name="attend")(lens, x, freq, gains, wqkv)
 
 def adam_step(weight, grad_sum, moment, second, rate, decay):
     moment_new = beta_one * moment + (1.0 - beta_one) * grad_sum
@@ -246,15 +397,22 @@
     x = tokens.reshape(S, D)
     cot = cotangent.reshape(S, D)
     gain_low = gains.astype(bf16)
-    wqkv = lax.all_gather(qkv_w.astype(bf16), "dp", axis=1, tiled=True)
-    gain_full = lax.all_gather(gain_low, "dp", axis=1, tiled=True).astype(f32)
-    wo = lax.all_gather(out_w.astype(bf16), "dp", axis=0, tiled=True)
-    wgu = lax.all_gather(gu_w.astype(bf16), "dp", axis=1, tiled=True)
-    wd = lax.all_gather(down_w.astype(bf16), "dp", axis=0, tiled=True)
-    gain8 = jnp.pad(gain_full, ((0, 6), (0, 0)))
     freq = 10000.0 ** (-jnp.arange(HD // 2, dtype=f32) / (HD // 2))
     freq = jnp.broadcast_to(freq[:, None], (HD // 2, 128))
-    qT, kT, vT, ob, oT, lse, cos, sin, segc, segr = attn_fwd(seg_lens, x, gain8, freq, wqkv)
+    n_dp, n_rep = lax.axis_size("dp"), lax.axis_size("rep")
+    if can_gather(n_dp, n_rep, qkv_w.shape[1], out_w.shape[0], gu_w.shape[1], down_w.shape[0]):
+        piece = jnp.pad(gain_low.astype(f32), ((0, 6), (0, 128 - gains.shape[1])))
+        qT, kT, vT, oT, lse, cos, sin, segc, segr, gain8, wqkv, wo, wgu, wd = ka(
+            n_dp, n_rep, seg_lens, x, freq, piece, qkv_w, out_w, gu_w, down_w)
+    else:
+        wqkv = lax.all_gather(qkv_w.astype(bf16), "dp", axis=1, tiled=True)
+        gain_full = lax.all_gather(gain_low, "dp", axis=1, tiled=True).astype(f32)
+        wo = lax.all_gather(out_w.astype(bf16), "dp", axis=0, tiled=True)
+        wgu = lax.all_gather(gu_w.astype(bf16), "dp", axis=1, tiled=True)
+        wd = lax.all_gather(down_w.astype(bf16), "dp", axis=0, tiled=True)
+        gain8 = jnp.pad(gain_full, ((0, 6), (0, 0)))
+        qT, kT, vT, oT, lse, cos, sin, segc, segr = attn_fwd(seg_lens, x, gain8, freq, wqkv)
+    ob = oT.T
     output, dmid, dob, dobT, dwo, dwgu, dwd = mlp(x, ob, oT, cot, wo, wgu, wd, gain8)
     input_grad, dwqkv = attn_bwd(x, gain8, wqkv, dmid, qT, kT, vT, dob, dobT, oT, lse, cos, sin, segc, segr)
 

time: 558 us -> 490 us (0.88)
  waiting for transfers between devices: 248 us -> 151 us
  Pallas kernels: 140 us -> 183 us
  blocking collectives: 136 us -> 126 us
    all_gather x4 -> x0, waiting for transfers between devices: 96.6 us -> none  [the longest x1 47.9 us: per_device(): wgu = lax.all_gather(gu_w.astype(bf16), 'dp', axis=1, tiled=True)]
    pallas_call x1, Pallas kernels: 36.2 us -> 79.2 us  [ka(): pl.pallas_call(functools.partial(ka_body, (n_dp, n_rep)), in_specs=[SM, V...]
    all_gather x1 -> x0, blocking collectives: 10.2 us -> none  [per_device(): gain_full = lax.all_gather(gain_low, 'dp', axis=1, tiled=True).astype(f32)]
  transfers between devices with their start and end apart: 8 -> 4, of which waited for: 6 -> 3; matrix products, arithmetic and copies ran while one was open for 1% -> 0% of each run, Pallas kernels for 16% -> 11%
where the time goes in v2:
time: 490 us
  Pallas kernels  183 us (37%)
  waiting for transfers between devices  151 us (31%)
  blocking collectives  126 us (26%)
  between operations  14 us (3%)
  other arithmetic  11 us (2%)
    reduce_scatter x4, waiting for transfers between devices, owned(): part = lax.psum_scatter(grad, 'dp', scatter_dimension=axis, tiled=True)  150 us
    psum x1, blocking collectives, owned(): return lax.psum(part.astype(f32), 'rep')  126 us
    pallas_call x1, Pallas kernels, ka(): pl.pallas_call(functools.partial(ka_body, (n_dp, n_rep)), in_specs=[SM, V...  79.2 us
    pallas_call x1, Pallas kernels, attn_bwd(): pl.pallas_call(attn_bwd_body, in_specs=[VM] * 15, out_specs=[VM] * 2, out...  52.1 us
    pallas_call x1, Pallas kernels, mlp(): pl.pallas_call(functools.partial(mlp_kernel, T), grid=(FF // FC,), in_spe...  51.9 us
    sub x5, other arithmetic, adam_step(): weight - rate * (moment_hat / (jnp.sqrt(second_hat) + adam_eps) + decay *...  10.3 us
  transfers between devices with their start and end apart: 4, of which 3 were waited for; matrix products, arithmetic and copies ran while one was open for 0% of the time, Pallas kernels for 11%

profile of v2, /device:TPU:0, one launch (start us, length us, event | category | flops | bytes accessed | tf_op | source)
XLA Modules:
  0.0 490.2 jit_solution(15964255377503592260)
XLA Ops:
  7.2 0.0 reduce-scatter.7.cloned.1.call-start
  7.2 0.7 convert_convert_fusion
  7.9 0.6 pad.4.gain_ref
  8.5 0.7 broadcast_in_dim.2.freq_ref
  9.2 79.2 %gather_attend.1 = (bf16[768,1024]{1,0:T(8,128)(2,1)}, bf16[768,1024]{1,0:T(8,128)(2,1)}, bf16[768,1024]{1,0:T(8,128)(2,1)}, bf16[768,1024]{1,0:T(8,128)(2,1)}, ...) custom-call(s32[1,5]{1,0:T(1,128)} %lens_ref.1, ...), custom_call_target="tpu_custom_call" | custom-call | flops 12000000000 | bytes 30000000 | tf_op jit(solution)/shard_map/gather_attend/pallas_call | solution.py:359
  88.4 2.6 copy.35
  91.0 51.9 %mlp.1 = (f32[1024,768]{1,0:T(8,128)}, f32[1024,768]{1,0:T(8,128)}, bf16[1024,768]{1,0:T(8,128)(2,1)}, bf16[768,1024]{1,0:T(8,128)(2,1)}, bf16[768,768]{1,0:T(8,...) custom-call(bf16[1024,768]{1,0:T(8,128)(2,1)} %bitcast.10, bf16[1024,768]{1,0:T(8,128)(2,1)} %bitcast.12, ...), custom_call_target="tpu_custom_call" | custom-call | tf_op jit(solution)/shard_map/mlp/pallas_call | solution.py:76
  142.9 0.0 reduce-scatter.7.cloned.1.call-update
  142.9 0.0 reduce-scatter.11.cloned.1.call-start
  143.0 0.7 reduce-scatter.11.cloned.1.call-update
  143.7 0.2 reduce-scatter.5.cloned.1.call-start
  143.9 52.1 %attn_bwd.1 = (f32[1024,768]{1,0:T(8,128)}, bf16[3,768,768]{2,1,0:T(8,128)(2,1)}) custom-call(bf16[1024,768]{1,0:T(8,128)(2,1)} %bitcast.11, f32[8,768]{1,0:T(8,128)} %get-tuple-element.44.gain_ref, bf16[3,768,768]{2,1,0:T(8,128)(2,1)} %get-tuple-element.46.wqkv_ref, f32[1024,768]{1,0:T(8,128)} %get-tuple-element.47.dmid_ref, ...), custom_call_target="tpu_custom_call" | custom-call | tf_op jit(solution)/shard_map/attn_bwd/pallas_call | solution.py:173
  196.0 0.0 reduce-scatter.5.cloned.1.call-update
  196.0 0.0 reduce-scatter.9.cloned.1.call-start
  196.1 0.5 reduce-scatter.9.cloned.1.call-update
  196.6 0.0 copy-start.3
  196.7 0.0 reduce-scatter.7.cloned.1.call-done
  196.7 33.2 %reduce-scatter.11.cloned.1.call-done = bf16[256,768]{1,0:T(8,128)(2,1)} async-done(((bf16[2048,768]{1,0:T(8,128)(2,1)}), bf16[256,768]{1,0:T(8,128)(2,1)}) %reduce-scatter.11.cloned.1.call-update) | async-done | bytes 393232 | tf_op jit(solution)/shard_map/reduce_scatter | solution.py:420
  229.9 51.6 %reduce-scatter.5.cloned.1.call-done = bf16[3,96,768]{2,1,0:T(8,128)(2,1)} async-done(((bf16[3,768,768]{2,1,0:T(8,128)(2,1)}), bf16[3,96,768]{2,1,0:T(8,128)(2,1)}) %reduce-scatter.5.cloned.1.call-update) | async-done | bytes 442384 | tf_op jit(solution)/shard_map/reduce_scatter | solution.py:420
  281.6 65.0 %reduce-scatter.9.cloned.1.call-done = bf16[2,96,2048]{2,1,0:T(8,128)(2,1)} async-done(((bf16[2,768,2048]{2,1,0:T(8,128)(2,1)}), bf16[2,96,2048]{2,1,0:T(8,128)(2,1)}) %reduce-scatter.9.cloned.1.call-update) | async-done | bytes 786448 | tf_op jit(solution)/shard_map/reduce_scatter | solution.py:420
  346.5 126.0 %all-reduce.3 = (f32[3,96,768]{2,1,0:T(8,128)}, f32[96,768]{1,0:T(8,128)}, f32[2,96,2048]{2,1,0:T(8,128)S(1)}, f32[256,768]{1,0:T(8,128)}) all-reduce(bf16[3,96,768]{2,1,0:T(8,128)(2,1)} %reduce-scatter.5.cloned.1.call-done, bf16[96,768]{1,0:T(8,128)(2,1)} %reduce-scatter.7.cloned.1.call-done, ...), channel_id=1, replica_groups=mesh['dp'=8,'rep'=4] {'rep'}, use_global_device_ids=true, to_apply=%region_1.2 | all-reduce | flops 884736 | bytes 5308416 | tf_op jit(solution)/shard_map/psum | solution.py:421
  472.6 0.0 copy-start.2
  472.6 3.6 multiply_subtract_fusion.1
  476.3 0.0 copy-start.9
  476.3 0.0 copy-start.12
  476.3 0.0 copy-start.7
  476.3 3.2 multiply_subtract_fusion
  479.6 1.0 multiply_subtract_fusion.3
  480.7 0.2 copy-done.5
  480.9 0.4 copy-done.6
  481.3 1.8 multiply_subtract_fusion.2
  483.1 0.6 multiply_subtract_fusion.4
  (27 shorter events, 0.1 us)
Async XLA Ops:
  7.2 189.5 %reduce-scatter.7.cloned.1.call-start = ((), (), s32[]{:S(2)}) async-start(), calls=%async_computation.5 | async-start | bytes 1327104 | tf_op jit(solution)/shard_map/reduce_scatter | solution.py:420
  142.9 87.0 %reduce-scatter.11.cloned.1.call-start = ((), (), s32[]{:S(2)}) async-start(), calls=%async_computation.7 | async-start | bytes 3538944 | tf_op jit(solution)/shard_map/reduce_scatter | solution.py:420
  143.7 137.9 %reduce-scatter.5.cloned.1.call-start = ((), (), s32[]{:S(2)}) async-start(), calls=%async_computation.4 | async-start | bytes 3981312 | tf_op jit(solution)/shard_map/reduce_scatter | solution.py:420
  196.0 150.5 %reduce-scatter.9.cloned.1.call-start = ((), (), s32[]{:S(2)}) async-start(), calls=%async_computation.6 | async-start | bytes 7077888 | tf_op jit(solution)/shard_map/reduce_scatter | solution.py:420
  196.6 275.9 %copy-start.3 = (f32[3,96,768]{2,1,0:T(8,128)S(1)}, f32[3,96,768]{2,1,0:T(8,128)}, u32[]{:S(2)}) copy-start(f32[3,96,768]{2,1,0:T(8,128)} %qw_ref.1) | copy-start | bytes 2654212
  196.6 275.9 %copy-start.4 = (f32[3,96,768]{2,1,0:T(8,128)S(1)}, f32[3,96,768]{2,1,0:T(8,128)}, u32[]{:S(2)}) copy-start(f32[3,96,768]{2,1,0:T(8,128)} %param.27) | copy-start | bytes 2654212
  472.6 3.7 copy-start
  472.6 3.7 copy-start.1
  472.6 3.7 copy-start.2
  476.3 3.3 copy-start.9
  476.3 3.3 copy-start.10
  476.3 3.3 copy-start.11
  476.3 3.3 copy-start.12
  476.3 4.4 copy-start.7
  476.3 4.4 copy-start.8
  479.6 1.3 copy-start.5
  479.6 1.7 copy-start.6
  481.3 1.8 copy-start.13
  481.3 1.8 copy-start.14
  481.3 1.8 copy-start.15
Sparse Core Ops, SparseCore 0:
  143.1 36.8 reduce-scatter.6
  183.7 46.2 reduce-scatter.10
  233.4 48.0 reduce-scatter.4
  284.8 61.6 reduce-scatter.8

commit v3 on v2

--- a/solution.py
+++ b/solution.py
@@ -104,78 +104,6 @@
         start += past * lens_ref[0, s]
     return seg, slot - start
 
-def attn_bwd_body(x_ref, gain_ref, wqkv_ref, dmid_ref, qT_ref, kT_ref, vT_ref, dob_ref, dobT_ref, oT_ref, lse_ref, cos_ref, sin_ref, segc_ref, segr_ref,
-                  ig_ref, dw_ref, bias_s, k_s, v_s, q_s, dqT_s, dk_s, dv_s, dkT_s, h1T_s, B=256):
-    S, D = x_ref.shape
-    n = S // B
-    k_s[...] = kT_ref[...].T; v_s[...] = vT_ref[...].T; q_s[...] = qT_ref[...].T
-    dk_s[...] = jnp.zeros_like(dk_s); dv_s[...] = jnp.zeros_like(dv_s)
-    lane = lax.broadcasted_iota(jnp.int32, (B, 128), 1)
-    for i in range(n):
-        k0 = max(0, i-2)*B; nk = i*B + B - k0
-        q0 = i*B
-        kid = lax.broadcasted_iota(jnp.int32, (nk, B), 0) + k0
-        qid = lax.broadcasted_iota(jnp.int32, (nk, B), 1) + q0
-        ok = (segc_ref[k0:k0+nk, 0:1] == segr_ref[0:1, q0:q0+B]) & (kid <= qid)
-        bias_s[0:nk, :] = jnp.where(ok, 0.0, NEG)
-        @pl.loop(0, H//2)
-        def _(p):
-            cols = pl.ds(pl.multiple_of(p*128, 128), 128)
-            dv = None
-            for e in range(2):
-                rows = pl.ds(pl.multiple_of(p*128 + e*64, 64), 64)
-                mine = (lane < 64) if e == 0 else (lane >= 64)
-                dobz = jnp.where(mine, dob_ref[q0:q0+B, cols], 0).astype(bf16)
-                qz = jnp.where(mine, q_s[q0:q0+B, cols], 0).astype(bf16)
-                s = tn(kT_ref[rows, k0:k0+nk], qT_ref[rows, q0:q0+B]) + bias_s[0:nk, :]
-                pr = jnp.exp(s - lse_ref[pl.ds(p*2+e, 1), q0:q0+B])
-                dp = tn(vT_ref[rows, k0:k0+nk], dobT_ref[rows, q0:q0+B])
-                inner = jnp.sum(pr*dp, axis=0, keepdims=True)
-                ds = (pr*(dp - inner)).astype(bf16)
-                dve = nn(pr.astype(bf16), dobz)
-                dke = nn(ds, qz)
-                dqT_s[rows, q0:q0+B] = nn(kT_ref[rows, k0:k0+nk], ds) * 0.125
-                dv = dve if dv is None else dv + dve
-                dk = dke if e == 0 else dk + dke
-            dv_s[k0:k0+nk, cols] += dv
-            dk_s[k0:k0+nk, cols] += dk
-    @pl.loop(0, n)
-    def _(i):
-        t = pl.ds(pl.multiple_of(i*B, B), B)
-        c = cos_ref[:, t]; s = sin_ref[:, t]
-        dkT = dk_s[t, :].T
-        for src, dst in ((dqT_s[:, t], qT_ref), (dkT, kT_ref)):
-            for h in range(H):
-                a = src[h*HD:h*HD+32]; b = src[h*HD+32:h*HD+64]
-                dqT_s[h*HD:h*HD+32, t] = a*c + b*s
-                dqT_s[h*HD+32:h*HD+64, t] = b*c - a*s
-            if dst is qT_ref:
-                q_s[t, :] = dqT_s[:, t].astype(bf16).T
-            else:
-                k_s[t, :] = dqT_s[:, t].astype(bf16).T
-        dvb = dv_s[t, :].astype(bf16)
-        v_s[t, :] = dvb
-        gain = gain_ref[0:1, :]
-        xf = x_ref[t, :].astype(f32)
-        r = lax.rsqrt(jnp.mean(xf*xf, axis=-1, keepdims=True) + EPS)
-        xh = xf*r
-        h1T_s[:, t] = (xh*gain).astype(bf16).T
-        dh = nt(q_s[t, :], wqkv_ref[0]) + nt(k_s[t, :], wqkv_ref[1]) + nt(dvb, wqkv_ref[2])
-        w = dh*gain
-        ig_ref[t, :] = dmid_ref[t, :] + r*(w - xh*jnp.mean(w*xh, axis=-1, keepdims=True))
-    dw_ref[0] = nn(h1T_s[...], q_s[...]).astype(bf16)
-    dw_ref[1] = nn(h1T_s[...], k_s[...]).astype(bf16)
-    dw_ref[2] = nn(h1T_s[...], v_s[...]).astype(bf16)
-
-def attn_bwd(x, gains, wqkv, dmid, qT, kT, vT, dob, dobT, oT, lse, cos, sin, segc, segr):
-    S, D = x.shape
-    sh = lambda s, d: jax.ShapeDtypeStruct(s, d)
-    return pl.pallas_call(attn_bwd_body,
-        in_specs=[VM]*15, out_specs=[VM]*2,
-        out_shape=[sh((S,D),f32), sh((3,D,D),bf16)],
-        scratch_shapes=[pltpu.VMEM((768,256),f32), pltpu.VMEM((S,D),bf16), pltpu.VMEM((S,D),bf16), pltpu.VMEM((S,D),bf16),
-                        pltpu.VMEM((D,S),f32), pltpu.VMEM((S,D),f32), pltpu.VMEM((S,D),f32), pltpu.VMEM((8,128),f32), pltpu.VMEM((D,S),bf16)],
-        compiler_params=pltpu.CompilerParams(vmem_limit_bytes=62*2**20), name="attn_bwd")(x, gains, wqkv, dmid, qT, kT, vT, dob, dobT, oT, lse, cos, sin, segc, segr)
 
 MESH = pl.DeviceIdType.MESH
 
@@ -382,6 +310,278 @@
         scratch_shapes=[pltpu.VMEM((768,256),f32)],
         compiler_params=pltpu.CompilerParams(vmem_limit_bytes=62*2**20), name="attend")(lens, x, freq, gains, wqkv)
 
+GW = 256
+
+def backward_attention(x_ref, gain_ref, w_ref, ig_s, ig_ready, ig_done, qT_ref, kT_ref, vT_ref, dob_ref, dobT_ref, lse_ref, cos_ref, sin_ref, segc_ref, segr_ref,
+                       dw_s, bias_s, q_s, dqT_s, dk_s, dv_s, g_s, h1T_s, hook):
+    S, D = x_ref.shape
+    n = S // B
+    gain = gain_ref[0:1, :]
+    hook("start")
+    blocks = []
+    at = 0
+    for i in range(n):
+        k0 = max(0, i-2)*B; nk = i*B + B - k0
+        q0 = i*B
+        kid = lax.broadcasted_iota(jnp.int32, (nk, B), 0) + k0
+        qid = lax.broadcasted_iota(jnp.int32, (nk, B), 1) + q0
+        ok = (segc_ref[k0:k0+nk, 0:1] == segr_ref[0:1, q0:q0+B]) & (kid <= qid)
+        bias_s[at:at+nk, :] = jnp.where(ok, 0.0, NEG)
+        blocks.append((q0, k0, nk, at)); at += nk
+    q_s[...] = qT_ref[...].T
+    @pl.loop(0, n)
+    def _(i):
+        t = pl.ds(pl.multiple_of(i*B, B), B)
+        xf = x_ref[t, :].astype(f32)
+        r = lax.rsqrt(jnp.mean(xf*xf, axis=-1, keepdims=True) + EPS)
+        h1T_s[:, t] = ((xf*r)*gain).astype(bf16).T
+    hook("ready")
+    lane = lax.broadcasted_iota(jnp.int32, (B, 128), 1)
+    @pl.loop(0, H//2)
+    def _(p):
+        cols = pl.ds(pl.multiple_of(p*128, 128), 128)
+        dk_s[...] = jnp.zeros_like(dk_s); dv_s[...] = jnp.zeros_like(dv_s)
+        for q0, k0, nk, at in blocks:
+            dv = dk = None
+            for e in range(2):
+                rows = pl.ds(pl.multiple_of(p*128 + e*64, 64), 64)
+                mine = (lane < 64) if e == 0 else (lane >= 64)
+                dobz = jnp.where(mine, dob_ref[q0:q0+B, cols], 0).astype(bf16)
+                qz = jnp.where(mine, q_s[q0:q0+B, cols], 0).astype(bf16)
+                s = tn(kT_ref[rows, k0:k0+nk], qT_ref[rows, q0:q0+B]) + bias_s[at:at+nk, :]
+                pr = jnp.exp(s - lse_ref[pl.ds(p*2+e, 1), q0:q0+B])
+                dp = tn(vT_ref[rows, k0:k0+nk], dobT_ref[rows, q0:q0+B])
+                inner = jnp.sum(pr*dp, axis=0, keepdims=True)
+                ds = (pr*(dp - inner)).astype(bf16)
+                dve = nn(pr.astype(bf16), dobz)
+                dke = nn(ds, qz)
+                dqT_s[e*64:e*64+64, q0:q0+B] = nn(kT_ref[rows, k0:k0+nk], ds) * 0.125
+                dv = dve if dv is None else dv + dve
+                dk = dke if dk is None else dk + dke
+            dv_s[k0:k0+nk, :] += dv
+            dk_s[k0:k0+nk, :] += dk
+        c = cos_ref[...]; s = sin_ref[...]
+        for j, src in ((0, dqT_s[...]), (1, dk_s[...].T)):
+            parts = []
+            for e in range(2):
+                a = src[e*HD:e*HD+32]; b = src[e*HD+32:e*HD+64]
+                parts += [a*c + b*s, b*c - a*s]
+            g_s[j, :, cols] = jnp.concatenate(parts, axis=0).astype(bf16).T
+        g_s[2, :, cols] = dv_s[...].astype(bf16)
+        @pl.when(lax.rem(p, 2) == 1)
+        def _():
+            g = lax.div(p, 2)
+            wide = pl.ds(pl.multiple_of(g*GW, GW), GW)
+            for j in range(3):
+                dw_s[g, j] = nn(h1T_s[...], g_s[j, :, wide]).astype(bf16)
+        for k in range(H//2):
+            @pl.when(p == k)
+            def _():
+                hook(k)
+    ig_ready()
+    for i in range(n):
+        t = pl.ds(i*B, B)
+        xf = x_ref[t, :].astype(f32)
+        r = lax.rsqrt(jnp.mean(xf*xf, axis=-1, keepdims=True) + EPS)
+        xh = xf*r
+        dh = nt(g_s[0, t, :], w_ref[0]) + nt(g_s[1, t, :], w_ref[1]) + nt(g_s[2, t, :], w_ref[2])
+        w = dh*gain
+        ig_s[t, :] += r*(w - xh*jnp.mean(w*xh, axis=-1, keepdims=True))
+        ig_done(i, t)
+        hook("tile%d" % i)
+
+def scratch_bwd(S, D):
+    n = S // B
+    area = sum(min(i+1, 3) for i in range(n))*B
+    return [pltpu.VMEM((D//GW, 3, D, GW), bf16), pltpu.VMEM((area, B), f32), pltpu.VMEM((S, D), bf16), pltpu.VMEM((128, S), f32),
+            pltpu.VMEM((S, 128), f32), pltpu.VMEM((S, 128), f32), pltpu.VMEM((3, S, D), bf16), pltpu.VMEM((D, S), bf16)]
+
+def bwd_local_body(x_ref, gain_ref, w_ref, dmid_ref, qT_ref, kT_ref, vT_ref, dob_ref, dobT_ref, lse_ref, cos_ref, sin_ref, segc_ref, segr_ref,
+                   ig_ref, dw_ref, bias_s, q_s, dqT_s, dk_s, dv_s, g_s, h1T_s):
+    ig_ref[...] = dmid_ref[...]
+    backward_attention(x_ref, gain_ref, w_ref, ig_ref, lambda: None, lambda i, t: None, qT_ref, kT_ref, vT_ref, dob_ref, dobT_ref, lse_ref, cos_ref, sin_ref,
+                       segc_ref, segr_ref, dw_ref, bias_s, q_s, dqT_s, dk_s, dv_s, g_s, h1T_s, lambda at: None)
+
+def attn_bwd(x, gains, wqkv, dmid, qT, kT, vT, dob, dobT, lse, cos, sin, segc, segr):
+    S, D = x.shape
+    sh = lambda s, d: jax.ShapeDtypeStruct(s, d)
+    ig, dw = pl.pallas_call(bwd_local_body,
+        in_specs=[VM]*14, out_specs=[VM]*2,
+        out_shape=[sh((S,D),f32), sh((D//GW,3,D,GW),bf16)],
+        scratch_shapes=scratch_bwd(S, D)[1:],
+        compiler_params=pltpu.CompilerParams(vmem_limit_bytes=62*2**20), name="attend_back")(x, gains, wqkv, dmid, qT, kT, vT, dob, dobT, lse, cos, sin, segc, segr)
+    return ig, jnp.moveaxis(dw, 0, 2).reshape(3, D, D)
+
+class Reduce:
+    N = 13
+    def __init__(self, u, piece, other, own_load, rs, rx, r2, zr, tot, out, send, recv):
+        self.u, self.piece, self.other, self.own_load = u, piece, other, own_load
+        self.rs, self.rx, self.r2, self.zr, self.tot, self.out, self.send, self.recv = rs, rx, r2, zr, tot, out, send, recv
+        self.d, self.z, self.sib, self.xn, self.yn, self.xy = places()
+        self.rows = rs.shape[-2]; self.half = self.rows // 2
+        self.inner = (self.z == 1) | (self.z == 2)
+    def cut(self, ref, h):
+        s = slice(0, self.half) if h == 0 else slice(self.half, self.rows)
+        return ref.at[..., s, :]
+    def copy(self, k, src, dst, dev):
+        return pltpu.make_async_remote_copy(src_ref=src, dst_ref=dst, send_sem=self.send.at[self.u, k], recv_sem=self.recv.at[self.u, k],
+                                            device_id=dev, device_id_type=MESH)
+    def s_copy(self, j): return self.copy(j, self.other(j), self.rs.at[j], (self.sib, self.z))
+    def x_copies(self):
+        X, Y = (self.xn, self.z), (self.yn, self.z)
+        return [self.copy(4, self.half_of(1, 0), self.cut(self.rx.at[0], 0), X), self.copy(5, self.half_of(3, 0), self.cut(self.rx.at[1], 0), X),
+                self.copy(6, self.half_of(2, 1), self.cut(self.rx.at[0], 1), Y), self.copy(7, self.half_of(3, 1), self.cut(self.rx.at[1], 1), Y)]
+    def half_of(self, j, h): return self.piece(j, h)
+    def y_copies(self):
+        return [self.copy(8, self.half_of(2, 0), self.cut(self.r2, 0), (self.yn, self.z)), self.copy(9, self.half_of(1, 1), self.cut(self.r2, 1), (self.xn, self.z))]
+    def z_copy(self, k):
+        zn = (self.d, flip(self.z, 1))
+        if k == 0: return self.copy(10, self.piece(0, None), self.zr.at[0], zn)
+        if k == 1: return self.copy(11, self.zr.at[0], self.zr.at[1], (self.d, 3 - self.z))
+        return self.copy(12, self.tot, self.tot, zn)
+    def add(self, dst, *refs):
+        lead = dst.shape[0] if len(dst.shape) == 3 else None
+        def one(i):
+            g = (lambda r: r[...]) if i is None else (lambda r: r[i])
+            v = g(refs[0]).astype(f32)
+            for r in refs[1:]: v += g(r).astype(f32)
+            if i is None: dst[...] = v.astype(bf16)
+            else: dst[i] = v.astype(bf16)
+        if lead is None: one(None)
+        else:
+            for i in range(lead): one(i)
+    def start_s(self):
+        for j in range(4): self.s_copy(j).start()
+        if self.own_load:
+            for j in range(4): self.own_load(j).start()
+    def s2x(self):
+        for j in (3, 1, 2, 0):
+            self.s_copy(j).wait_recv()
+            if self.own_load: self.own_load(j).wait()
+            p = self.piece(j, None)
+            self.add(p, p, self.rs.at[j])
+        for c in self.x_copies(): c.start()
+    def x2y(self):
+        cs = self.x_copies()
+        for c in cs: c.wait_recv()
+        for j, h, r in ((2, 0, 1), (1, 1, 1)):
+            p = self.piece(j, h)
+            self.add(p, p, self.cut(self.rx.at[r], h))
+        for c in self.y_copies(): c.start()
+        p = self.piece(0, None)
+        self.add(p, p, self.rx.at[0])
+    def y2z(self):
+        for c in self.y_copies(): c.wait_recv()
+        p = self.piece(0, None)
+        self.add(p, p, self.r2)
+        @pl.when(jnp.logical_not(self.inner))
+        def _(): self.z_copy(0).start()
+    def z2(self):
+        @pl.when(self.inner)
+        def _():
+            self.z_copy(0).wait_recv()
+            self.add(self.zr.at[0], self.zr.at[0], self.piece(0, None))
+            self.z_copy(1).start()
+    def z3(self):
+        @pl.when(self.inner)
+        def _():
+            self.z_copy(1).wait_recv()
+            self.add(self.tot, self.zr.at[0], self.zr.at[1])
+            self.z_copy(2).start()
+            self.out().start()
+    def last(self):
+        @pl.when(jnp.logical_not(self.inner))
+        def _():
+            self.z_copy(2).wait_recv()
+            self.out().start()
+    def drain(self):
+        for j in range(4): self.s_copy(j).wait_send()
+        for c in self.x_copies() + self.y_copies(): c.wait_send()
+        @pl.when(self.inner)
+        def _():
+            self.z_copy(1).wait_send(); self.z_copy(2).wait_send()
+        @pl.when(jnp.logical_not(self.inner))
+        def _(): self.z_copy(0).wait_send()
+        self.out().wait()
+
+def kc_body(x_ref, gain_ref, w_ref, qT_ref, kT_ref, vT_ref, dob_ref, dobT_ref, lse_ref, cos_ref, sin_ref, segc_ref, segr_ref, dmid_ref, dgu_ref, ddn_ref, dou_ref,
+            ig_o, gq_o, ggu_o, gdn_o, gou_o,
+            dw_s, bias_s, q_s, dqT_s, dk_s, dv_s, g_s, h1T_s, ig_s,
+            gu_p, gu_rs, gu_rx, gu_r2, gu_z, gu_t, dn_p, dn_rs, dn_rx, dn_r2, dn_z, dn_t, ou_p, ou_rs, ou_rx, ou_r2, ou_z, ou_t, q_rs, q_rx, q_r2, q_z, q_t,
+            send, recv, loc):
+    S, D = x_ref.shape
+    n = S // B
+    d, z, sib, xn, yn, xy = places()
+    owners = [d, xn, yn, xy]
+    load = pltpu.make_async_copy(dmid_ref, ig_s, loc.at[0]); load.start()
+    def rows_of(ref, o, r, lead):
+        s = pl.ds(pl.multiple_of(o*r, 16), r)
+        return ref.at[:, s, :] if lead else ref.at[s, :]
+    def halves(r, h): return (0, r) if h is None else (h*(r//2), r//2)
+    units = []
+    for u, (ref, lead, p, rs, rx, r2, zr, tot, out) in enumerate(((ddn_ref, False, dn_p, dn_rs, dn_rx, dn_r2, dn_z, dn_t, gdn_o), (dgu_ref, True, gu_p, gu_rs, gu_rx, gu_r2, gu_z, gu_t, ggu_o),
+                                                                 (dou_ref, False, ou_p, ou_rs, ou_rx, ou_r2, ou_z, ou_t, gou_o))):
+        r = rs.shape[-2]
+        def piece(j, h, p=p, r=r):
+            o, m = halves(r, h)
+            return p.at[j, ..., o:o+m, :]
+        other = lambda j, ref=ref, r=r, lead=lead: rows_of(ref, flip(owners[j], 1), r, lead)
+        own = lambda j, ref=ref, r=r, lead=lead, p=p, u=u: pltpu.make_async_copy(rows_of(ref, owners[j], r, lead), p.at[j], loc.at[1 + u*4 + j])
+        fin = lambda tot=tot, out=out, u=u: pltpu.make_async_copy(tot, out, loc.at[16 + u])
+        units.append(Reduce(u, piece, other, own, rs, rx, r2, zr, tot, fin, send, recv))
+    r = q_rs.shape[-2]
+    for g in range(D//GW):
+        def piece(j, h, g=g):
+            o, m = halves(r, h)
+            return dw_s.at[g, :, pl.ds(pl.multiple_of(owners[j]*r + o, 16), m), :]
+        other = lambda j, g=g: rows_of(dw_s.at[g], flip(owners[j], 1), r, True)
+        fin = lambda g=g: pltpu.make_async_copy(q_t.at[g], gq_o.at[:, :, pl.ds(g*GW, GW)], loc.at[19 + g])
+        units.append(Reduce(3+g, piece, other, None, q_rs.at[g], q_rx.at[g], q_r2.at[g], q_z.at[g], q_t.at[g], fin, send, recv))
+    U = units
+    def hook(at):
+        if at == "start":
+            greet([(sib, z), (xn, z), (yn, z), (d, flip(z, 1)), (d, 3 - z)])
+            U[0].start_s(); U[1].start_s(); U[2].start_s()
+        elif at == "ready": U[0].s2x()
+        elif at == 0: U[1].s2x(); U[2].s2x()
+        elif at == 1: U[3].start_s(); U[0].x2y()
+        elif at == 2: U[3].s2x()
+        elif at == 3: U[4].start_s(); U[1].x2y(); U[2].x2y()
+        elif at == 4: U[4].s2x(); U[0].y2z(); U[3].x2y()
+        elif at == 5: U[5].start_s(); U[0].z2(); U[1].y2z(); U[2].y2z(); U[4].x2y()
+        elif at == "tile0": U[5].s2x(); U[0].z3(); U[3].y2z()
+        elif at == "tile1": U[1].z2(); U[2].z2(); U[3].z2()
+        elif at == "tile2": U[4].y2z(); U[0].last()
+        elif at == "tile3":
+            U[5].x2y(); U[4].z2(); U[1].z3(); U[2].z3(); U[3].z3(); U[5].y2z(); U[4].z3(); U[5].z2(); U[5].z3()
+            for k in range(1, 6): U[k].last()
+    def ig_out(i): return pltpu.make_async_copy(ig_s.at[pl.ds(i*B, B), :], ig_o.at[pl.ds(i*B, B), :], loc.at[24 + i])
+    backward_attention(x_ref, gain_ref, w_ref, ig_s, load.wait, lambda i, t: ig_out(i).start(), qT_ref, kT_ref, vT_ref, dob_ref, dobT_ref, lse_ref, cos_ref, sin_ref,
+                       segc_ref, segr_ref, dw_s, bias_s, q_s, dqT_s, dk_s, dv_s, g_s, h1T_s, hook)
+    for u in U: u.drain()
+    for i in range(n): ig_out(i).wait()
+
+def kc(x, gains, wqkv, qT, kT, vT, dob, dobT, lse, cos, sin, segc, segr, dmid, dgu, ddn, dou, n_dp):
+    S, D = x.shape
+    FF = ddn.shape[0]
+    sh = lambda s, d: jax.ShapeDtypeStruct(s, d)
+    V = lambda *s: pltpu.VMEM(s, bf16)
+    def bufs(*piece): return [V(4, *piece), V(4, *piece), V(2, *piece), V(*piece), V(2, *piece), V(*piece)]
+    rq, rf = D//n_dp, FF//n_dp
+    G = D//GW
+    return pl.pallas_call(kc_body,
+        in_specs=[VM]*13 + [ANY]*4, out_specs=[ANY]*5,
+        out_shape=[sh((S,D),f32), sh((3,rq,D),bf16), sh((2,rq,FF),bf16), sh((rf,D),bf16), sh((rq,D),bf16)],
+        scratch_shapes=scratch_bwd(S, D) + [pltpu.VMEM((S,D),f32)] + bufs(2,rq,FF) + bufs(rf,D) + bufs(rq,D)
+            + [V(G,4,3,rq,GW), V(G,2,3,rq,GW), V(G,3,rq,GW), V(G,2,3,rq,GW), V(G,3,rq,GW)]
+            + [pltpu.SemaphoreType.DMA((3+G,13)), pltpu.SemaphoreType.DMA((3+G,13)), pltpu.SemaphoreType.DMA((32,))],
+        compiler_params=pltpu.CompilerParams(collective_id=1, has_side_effects=True, vmem_limit_bytes=62*2**20),
+        cost_estimate=pl.CostEstimate(flops=20*10**9, bytes_accessed=50*10**6, transcendentals=7*10**6),
+        name="attend_back_reduce")(x, gains, wqkv, qT, kT, vT, dob, dobT, lse, cos, sin, segc, segr, dmid, dgu, ddn, dou)
+
+def can_reduce(n_dp, n_rep, *rows):
+    return n_dp == 8 and n_rep == 4 and all(r % 32 == 0 for r in rows)
+
 def adam_step(weight, grad_sum, moment, second, rate, decay):
     moment_new = beta_one * moment + (1.0 - beta_one) * grad_sum
     second_new = beta_two * second + (1.0 - beta_two) * grad_sum * grad_sum
@@ -414,16 +614,20 @@
         qT, kT, vT, oT, lse, cos, sin, segc, segr = attn_fwd(seg_lens, x, gain8, freq, wqkv)
     ob = oT.T
     output, dmid, dob, dobT, dwo, dwgu, dwd = mlp(x, ob, oT, cot, wo, wgu, wd, gain8)
-    input_grad, dwqkv = attn_bwd(x, gain8, wqkv, dmid, qT, kT, vT, dob, dobT, oT, lse, cos, sin, segc, segr)
-
-    def owned(grad, axis):
-        part = lax.psum_scatter(grad, "dp", scatter_dimension=axis, tiled=True)
-        return lax.psum(part.astype(f32), "rep")
-
-    g_down = owned(dwd, 0)
-    g_gu = owned(dwgu, 1)
-    g_out = owned(dwo, 0)
-    g_qkv = owned(dwqkv, 1)
+    if can_reduce(n_dp, n_rep, qkv_w.shape[1], out_w.shape[0], gu_w.shape[1], down_w.shape[0]):
+        input_grad, g_qkv, g_gu, g_down, g_out = kc(x, gain8, wqkv, qT, kT, vT, dob, dobT, lse, cos, sin, segc, segr, dmid, dwgu, dwd, dwo, n_dp)
+        g_qkv, g_gu, g_down, g_out = (g.astype(f32) for g in (g_qkv, g_gu, g_down, g_out))
+    else:
+        input_grad, dwqkv = attn_bwd(x, gain8, wqkv, dmid, qT, kT, vT, dob, dobT, lse, cos, sin, segc, segr)
+
+        def owned(grad, axis):
+            part = lax.psum_scatter(grad, "dp", scatter_dimension=axis, tiled=True)
+            return lax.psum(part.astype(f32), "rep")
+
+        g_down = owned(dwd, 0)
+        g_gu = owned(dwgu, 1)
+        g_out = owned(dwo, 0)
+        g_qkv = owned(dwqkv, 1)
     gain_f = gain_low.astype(f32)
     g_gain = jnp.stack([
         jnp.sum(g_qkv * qkv_w.astype(bf16).astype(f32), axis=(0, 2)) / gain_f[0],

time: 490 us -> 276 us (0.56)
  waiting for transfers between devices: 151 us -> 0 us
  blocking collectives: 126 us -> 0 us
  Pallas kernels: 183 us -> 257 us
  between operations: 14 us -> 0.88 us
    reduce_scatter x4 -> x0, waiting for transfers between devices: 150 us -> none  [owned(): part = lax.psum_scatter(grad, 'dp', scatter_dimension=axis, tiled=True)]
    psum x1 -> x0, blocking collectives: 126 us -> none  [owned(): return lax.psum(part.astype(f32), 'rep')]
    pallas_call x1, Pallas kernels: 52.1 us -> 125 us  [kc(): pl.pallas_call(kc_body, in_specs=[VM] * 13 + [ANY] * 4, out_specs=[ANY] *...]
  transfers between devices with their start and end apart: 4 -> 0, of which waited for: 3 -> 0; matrix products, arithmetic and copies ran while one was open for 0% -> 0% of each run, Pallas kernels for 11% -> 0%
where the time goes in v3:
time: 276 us
  Pallas kernels  257 us (93%)
  other arithmetic  11.6 us (4%)
  local copies, waits for them, and re-layouts  6.97 us (3%)
    pallas_call x1, Pallas kernels, kc(): pl.pallas_call(kc_body, in_specs=[VM] * 13 + [ANY] * 4, out_specs=[ANY] *...  125 us
    pallas_call x1, Pallas kernels, ka(): pl.pallas_call(functools.partial(ka_body, (n_dp, n_rep)), in_specs=[SM, V...  79.2 us
    pallas_call x1, Pallas kernels, mlp(): pl.pallas_call(functools.partial(mlp_kernel, T), grid=(FF // FC,), in_spe...  52 us
    sub x5, other arithmetic, adam_step(): weight - rate * (moment_hat / (jnp.sqrt(second_hat) + adam_eps) + decay *...  10.9 us

profile of v3, /device:TPU:0, one launch (start us, length us, event | category | flops | bytes accessed | tf_op | source)
XLA Modules:
  0.0 276.1 jit_solution(1690664634744408807)
XLA Ops:
  0.7 0.7 convert_convert_fusion
  1.4 0.6 pad.4.gain_ref
  2.0 0.7 broadcast_in_dim.2.freq_ref
  2.6 79.2 %gather_attend.1 = (bf16[768,1024]{1,0:T(8,128)(2,1)}, bf16[768,1024]{1,0:T(8,128)(2,1)}, bf16[768,1024]{1,0:T(8,128)(2,1)}, bf16[768,1024]{1,0:T(8,128)(2,1)}, ...) custom-call(s32[1,5]{1,0:T(1,128)} %lens_ref.1, ...), custom_call_target="tpu_custom_call" | custom-call | flops 12000000000 | bytes 30000000 | tf_op jit(solution)/shard_map/gather_attend/pallas_call | solution.py:287
  81.8 2.6 copy.35
  84.4 52.0 %mlp.1 = (f32[1024,768]{1,0:T(8,128)}, f32[1024,768]{1,0:T(8,128)}, bf16[1024,768]{1,0:T(8,128)(2,1)}, bf16[768,1024]{1,0:T(8,128)(2,1)}, bf16[768,768]{1,0:T(8,...) custom-call(bf16[1024,768]{1,0:T(8,128)(2,1)} %bitcast.13, bf16[1024,768]{1,0:T(8,128)(2,1)} %bitcast.9, ...), custom_call_target="tpu_custom_call" | custom-call | tf_op jit(solution)/shard_map/mlp/pallas_call | solution.py:76
  136.4 0.0 copy-start.13
  136.4 0.0 copy-start.14
  136.4 0.0 copy-start.9
  136.4 125.4 %attend_back_reduce.1 = (f32[1024,768]{1,0:T(8,128)}, bf16[3,96,768]{2,1,0:T(8,128)(2,1)}, bf16[2,96,2048]{2,1,0:T(8,128)(2,1)}, bf16[256,768]{1,0:T(8,128)(2,1)}, bf16[96,768]{1,0:T(8,128)(2,1)}) custom-call(bf16[1024,768]{1,0:T(8,128)(2,1)} %bitcast.14, f32[8,768]{1,0:T(8,128)} %get-tuple-element.47.gain_ref, ...), custom_call_target="tpu_custom_call" | custom-call | flops 20000000000 | bytes 50000000 | tf_op jit(solution)/shard_map/attend_back_reduce/pallas_call | solution.py:572
  261.9 0.0 copy-start.7
  261.9 0.0 copy-start.8
  261.9 2.1 multiply_subtract_fusion.3
  264.0 0.0 copy-done.9
  264.0 0.0 copy-done.8
  264.0 0.0 copy-start.4
  264.0 0.0 copy-start.5
  264.0 0.0 copy-start.6
  264.0 0.0 copy-start.11
  264.0 3.0 %multiply_subtract_fusion.2 = (f32[256,768]{1,0:T(8,128)}, f32[256,768]{1,0:T(8,128)}, f32[256,768]{1,0:T(8,128)}) fusion(f32[256,768]{1,0:T(8,128)S(1)} %copy-done.7, bf16[256,768]{1,0:T(8,128)(2,1)} %get-tuple-element.68, f32[256,768]{1,0:T(8,128)S(1)} %copy-done.8, f32[256,768]{1,0:T(8,128)S(1)} %copy-done.9), kind=kLoop, calls=%fused_computation.20 | loop fusion | flops 3145728 | bytes 5111808 | tf_op jit(solution)/shard_map/sub | solution.py:590
  267.0 0.0 copy-done.4
  267.0 0.0 copy-start.1
  267.0 0.0 copy-start.2
  267.0 0.0 copy-start.3
  267.1 2.1 multiply_subtract_fusion.1
  269.2 0.7 copy-done.2
  269.9 0.5 copy-done.3
  270.3 0.2 copy-done.10
  270.5 3.2 %multiply_subtract_fusion = (f32[2,96,2048]{2,1,0:T(8,128)}, f32[2,96,2048]{2,1,0:T(8,128)}, f32[2,96,2048]{2,1,0:T(8,128)}, f32[96]{0:T(128)S(1)}) fusion(f32[2,96,2048]{2,1,0:T(8,128)S(1)} %copy-done.1, bf16[2,96,2048]{2,1,0:T(8,128)(2,1)S(1)} %copy-done.10, f32[2,96,2048]{2,1,0:T(8,128)S(1)} %copy-done.2, f32[2,96,2048]{2,1,0:T(8,128)S(1)} %copy-done.3), kind=kLoop, calls=%fused_computation.7 | loop fusion | flops 7864224 | bytes 10224000 | tf_op jit(solution)/shard_map/sub | solution.py:590
  273.8 0.0 copy-done.15
  273.8 0.6 multiply_subtract_fusion.4
  274.4 1.7 copy.37
  (19 shorter events, 0.1 us)
Async XLA Ops:
  136.4 125.5 %copy-start.12 = (f32[96,768]{1,0:T(8,128)S(1)}, f32[96,768]{1,0:T(8,128)}, u32[]{:S(2)}) copy-start(f32[96,768]{1,0:T(8,128)} %ow_ref.1) | copy-start | bytes 884740
  136.4 125.5 %copy-start.13 = (f32[96,768]{1,0:T(8,128)S(1)}, f32[96,768]{1,0:T(8,128)}, u32[]{:S(2)}) copy-start(f32[96,768]{1,0:T(8,128)} %param.29) | copy-start | bytes 884740
  136.4 125.5 %copy-start.14 = (f32[96,768]{1,0:T(8,128)S(1)}, f32[96,768]{1,0:T(8,128)}, u32[]{:S(2)}) copy-start(f32[96,768]{1,0:T(8,128)} %param.28) | copy-start | bytes 884740
  136.4 127.6 %copy-start.9 = (f32[256,768]{1,0:T(8,128)S(1)}, f32[256,768]{1,0:T(8,128)}, u32[]{:S(2)}) copy-start(f32[256,768]{1,0:T(8,128)} %param.32) | copy-start | bytes 2359300
  261.9 2.1 copy-start.7
  261.9 2.1 copy-start.8
  264.0 3.0 %copy-start.4 = (f32[3,96,768]{2,1,0:T(8,128)S(1)}, f32[3,96,768]{2,1,0:T(8,128)}, u32[]{:S(2)}) copy-start(f32[3,96,768]{2,1,0:T(8,128)} %qw_ref.1) | copy-start | bytes 2654212
  264.0 3.0 %copy-start.5 = (f32[3,96,768]{2,1,0:T(8,128)S(1)}, f32[3,96,768]{2,1,0:T(8,128)}, u32[]{:S(2)}) copy-start(f32[3,96,768]{2,1,0:T(8,128)} %param.27) | copy-start | bytes 2654212
  264.0 3.0 %copy-start.6 = (f32[3,96,768]{2,1,0:T(8,128)S(1)}, f32[3,96,768]{2,1,0:T(8,128)}, u32[]{:S(2)}) copy-start(f32[3,96,768]{2,1,0:T(8,128)} %param.26) | copy-start | bytes 2654212
  264.0 3.0 %copy-start.11 = (bf16[3,96,768]{2,1,0:T(8,128)(2,1)S(1)}, bf16[3,96,768]{2,1,0:T(8,128)(2,1)}, u32[]{:S(2)}) copy-start(bf16[3,96,768]{2,1,0:T(8,128)(2,1)} %get-tuple-element.65) | copy-start | bytes 1327108
  267.0 2.1 copy-start.1
  267.0 2.8 %copy-start.2 = (f32[2,96,2048]{2,1,0:T(8,128)S(1)}, f32[2,96,2048]{2,1,0:T(8,128)}, u32[]{:S(2)}) copy-start(f32[2,96,2048]{2,1,0:T(8,128)} %param.31) | copy-start | bytes 4718596
  267.0 3.3 %copy-start.3 = (f32[2,96,2048]{2,1,0:T(8,128)S(1)}, f32[2,96,2048]{2,1,0:T(8,128)}, u32[]{:S(2)}) copy-start(f32[2,96,2048]{2,1,0:T(8,128)} %param.30) | copy-start | bytes 4718596
  267.1 3.5 %copy-start.10 = (bf16[2,96,2048]{2,1,0:T(8,128)(2,1)S(1)}, bf16[2,96,2048]{2,1,0:T(8,128)(2,1)}, u32[]{:S(2)}) copy-start(bf16[2,96,2048]{2,1,0:T(8,128)(2,1)} %get-tuple-element.67) | copy-start | bytes 2359300
  270.5 3.3 %copy-start.15 = (f32[2,96]{1,0:T(2,128)S(1)}, f32[2,96]{1,0:T(2,128)}, u32[]{:S(2)}) copy-start(f32[2,96]{1,0:T(2,128)} %param.25) | copy-start | bytes 2308
  270.5 3.3 %copy-start.16 = (f32[2,96]{1,0:T(2,128)S(1)}, f32[2,96]{1,0:T(2,128)}, u32[]{:S(2)}) copy-start(f32[2,96]{1,0:T(2,128)} %param.35) | copy-start | bytes 2308
  270.5 3.3 %copy-start.17 = (f32[2,96]{1,0:T(2,128)S(1)}, f32[2,96]{1,0:T(2,128)}, u32[]{:S(2)}) copy-start(f32[2,96]{1,0:T(2,128)} %param.34) | copy-start | bytes 2308
  270.5 3.9 %copy-start = (f32[1024,768]{1,0:T(8,128)S(1)}, f32[1024,768]{1,0:T(8,128)}, u32[]{:S(2)}) copy-start(f32[1024,768]{1,0:T(8,128)} %get-tuple-element.64) | copy-start | bytes 9437188
